TPU v7x, 32 devices: a whole 2x2x4 slice. The times are simulated.
32 devices in a mesh: wide: 8 (over z, y), narrow: 4 (over x, core).
Axes of the slice: x: 2, y: 2, z: 4, core: 2. Of those that a mesh axis runs over, the one named last changes fastest.
Arguments:
- inputs: bfloat16 [3, 8, 196, 1024], P(None, 'wide')
- image_sides: int32 [3, 8], P(None, 'wide'), may hold values from 5 to 7
- tile_cuts: int32 [3, 8, 2], P(None, 'wide'), may hold values from 2 to 4
- cotangent: bfloat16 [3, 8, 49, 2048], P(None, 'wide'), may hold values from -6 to 6
- w_reduce1: bfloat16 [1024, 512], replicated, may hold values from -0.1875 to 0.1875
- w_spatial1: bfloat16 [9, 512, 512], replicated, may hold values from -0.09375 to 0.09375
- w_expand1: bfloat16 [512, 2048], replicated, may hold values from -0.25 to 0.25
- w_project1: bfloat16 [1024, 2048], replicated, may hold values from -0.1875 to 0.1875
- w_reduce2: bfloat16 [2048, 512], replicated, may hold values from -0.125 to 0.125
- w_spatial2: bfloat16 [9, 512, 512], replicated, may hold values from -0.09375 to 0.09375
- w_expand2: bfloat16 [512, 2048], replicated, may hold values from -0.25 to 0.25
- norm_gains: float32 [8192], replicated, may hold values from 0.1 to 1.9
- norm_biases: float32 [8192], replicated, may hold values from -3 to 3
Outputs:
- block_output: bfloat16 [3, 8, 49, 2048], P(None, 'wide', None, 'narrow')
- input_gradient: bfloat16 [3, 8, 196, 1024], P(None, 'wide', None, 'narrow')
- grad_reduce1: float32 [1024, 512], P('wide', 'narrow')
- grad_spatial1: float32 [9, 512, 512], P(None, 'wide', 'narrow')
- grad_expand1: float32 [512, 2048], P('wide', 'narrow')
- grad_project1: float32 [1024, 2048], P('wide', 'narrow')
- grad_reduce2: float32 [2048, 512], P('wide', 'narrow')
- grad_spatial2: float32 [9, 512, 512], P(None, 'wide', 'narrow')
- grad_expand2: float32 [512, 2048], P('wide', 'narrow')
- grad_gains: float32 [8192], P(('wide', 'narrow'))
- grad_biases: float32 [8192], P(('wide', 'narrow'))
- rms_values: float32 [4], replicated
Inputs may be any that keep to these rules, and one draw needn't show every extreme that they name: The valid cells of image k are the top left image_sides x image_sides cells of the output grid and the top left 2 * image_sides x 2 * image_sides cells of the input grid.
All inputs are finite; a program needn't handle non-finite values.
Results may differ from a plain program's by a relative error of at most 0.02.
Values may be sent and summed in bfloat16 or wider, within the bound.
A program may use at most 448 MiB of HBM per device.

v0:
```python
import math

import jax
import jax.numpy as jnp
from jax import lax
from jax.sharding import PartitionSpec as P

HALF = 7


EPSILON = 1e-05
TAP_STEPS = ((-1, -1), (-1, 0), (-1, 1), (0, -1), (0, 0), (0, 1), (1, -1), (1, 0), (1, 1))
OWNED_SETS = ((0, 1), (2, 3, 4), (5,), (6,))


def shortened(shard):

    def short(part):
        return part.astype(jnp.bfloat16) if part.dtype == jnp.float32 else part

    return jax.tree.map(short, shard)


def from_behind(shard, axis, by):
    size = lax.axis_size(axis)
    pairs = [(i, i + by) for i in range(size) if 0 <= i + by < size]
    return lax.ppermute(shard, axis, pairs)


def smooth(values):
    return jax.nn.gelu(values, approximate=True)


def smooth_back(values, upstream):
    return jax.vjp(smooth, values)[1](upstream)[0]


def pixel_masks(side_list, half_side):
    full_side = 2 * half_side
    full_cells = jnp.arange(full_side * full_side, dtype=jnp.int32)[None, :]
    full_limit = 2 * side_list[:, None]
    full_valid = (
        ((full_cells // full_side < full_limit) & (full_cells % full_side < full_limit))
        .astype(jnp.float32)
        .reshape(-1, 1)
    )
    half_cells = jnp.arange(half_side * half_side, dtype=jnp.int32)[None, :]
    half_limit = side_list[:, None]
    half_valid = (
        ((half_cells // half_side < half_limit) & (half_cells % half_side < half_limit))
        .astype(jnp.float32)
        .reshape(-1, 1)
    )
    return (full_valid, half_valid)


def tile_weights(cut_list, half_side):
    position = jnp.arange(half_side, dtype=jnp.int32)[None, :]
    cut_row = cut_list[:, 0:1]
    cut_col = cut_list[:, 1:2]
    tap_masks = []
    for row_step, col_step in TAP_STEPS:
        row_same = (position + row_step >= cut_row) == (position >= cut_row)
        col_same = (position + col_step >= cut_col) == (position >= cut_col)
        tap_masks.append((row_same[:, :, None] & col_same[:, None, :]).reshape(-1))
    return jnp.stack(tap_masks, axis=-1).astype(jnp.float32)[..., None]


def strided_cols(feature_grid, half_side):
    padded = jnp.pad(feature_grid, ((0, 0), (1, 1), (1, 1), (0, 0)))
    pieces = [
        padded[
            :,
            1 + row_step : 1 + row_step + 2 * half_side : 2,
            1 + col_step : 1 + col_step + 2 * half_side : 2,
            :,
        ]
        for row_step, col_step in TAP_STEPS
    ]
    joined = jnp.concatenate(pieces, axis=-1)
    return joined.reshape(-1, joined.shape[-1])


def tile_cols(flat_rows, tap_masks, images, half_side):
    channels = flat_rows.shape[-1]
    feature_grid = flat_rows.reshape(images, half_side, half_side, channels)
    padded = jnp.pad(feature_grid, ((0, 0), (1, 1), (1, 1), (0, 0)))
    pieces = [
        padded[
            :, 1 + row_step : 1 + row_step + half_side, 1 + col_step : 1 + col_step + half_side, :
        ]
        for row_step, col_step in TAP_STEPS
    ]
    stacked = jnp.stack(pieces, axis=3).reshape(-1, 9, channels)
    return (stacked * tap_masks.astype(flat_rows.dtype)).reshape(-1, 9 * channels)


def store_slot(store, value, index, limit):
    inside = (index >= 0) & (index < limit)
    place_at = jnp.clip(index, 0, limit - 1)
    return lax.dynamic_update_index_in_dim(
        store, jnp.where(inside, value, store[place_at]), place_at, 0
    )


def weight_product(left, right):
    return jnp.einsum("rc,rd->cd", left, right, preferred_element_type=jnp.float32)


def block_layout(grad, wide_count, segments):
    if grad.ndim == 2:
        rows, cols = grad.shape
        shaped = grad.reshape(wide_count, rows // wide_count, segments, cols // segments)
        return shaped.transpose(0, 2, 1, 3).reshape(wide_count, segments, -1)
    taps, rows, cols = grad.shape
    shaped = grad.reshape(taps, wide_count, rows // wide_count, segments, cols // segments)
    return shaped.transpose(1, 3, 0, 2, 4).reshape(wide_count, segments, -1)


def shard_shape(grad, wide_count, segments):
    if grad.ndim == 2:
        return (grad.shape[0] // wide_count, grad.shape[1] // segments)
    return (grad.shape[0], grad.shape[1] // wide_count, grad.shape[2] // segments)


def replace_at(items, index, value):
    return items[:index] + (value,) + items[index + 1 :]


def shards(
    inputs,
    image_sides,
    tile_cuts,
    cotangent,
    w_reduce1,
    w_spatial1,
    w_expand1,
    w_project1,
    w_reduce2,
    w_spatial2,
    w_expand2,
    norm_gains,
    norm_biases,
):
    segments = lax.axis_size("narrow")
    section = lax.axis_index("narrow")
    micro_count = inputs.shape[0]
    images = inputs.shape[1]
    in_width = w_reduce1.shape[0]
    mid_width = w_reduce1.shape[1]
    out_width = w_expand1.shape[1]
    half_side = HALF
    full_side = 2 * half_side
    half_rows = images * half_side * half_side
    full_rows = images * full_side * full_side
    stat_width = 2 * out_width
    first_matrix = w_spatial1.reshape(9 * mid_width, mid_width)
    second_matrix = w_spatial2.reshape(9 * mid_width, mid_width)
    starts = (
        0,
        mid_width,
        2 * mid_width,
        2 * mid_width + 2 * out_width,
        3 * mid_width + 2 * out_width,
        4 * mid_width + 2 * out_width,
    )
    widths = (mid_width, mid_width, 2 * out_width, mid_width, mid_width, out_width)
    carry_length = max(
        full_rows * mid_width + half_rows * mid_width + 2 * mid_width + 2,
        half_rows * (2 * out_width + mid_width) + 2 * out_width + mid_width + 2,
        half_rows * (mid_width + out_width),
    )
    empty_mid = jnp.zeros((half_rows, mid_width), jnp.bfloat16)
    empty_out = jnp.zeros((half_rows, out_width), jnp.bfloat16)
    empty_final = jnp.zeros((half_rows, out_width), jnp.float32)
    empty_squares = jnp.zeros((4,), jnp.float32)
    empty_input = jnp.zeros((images, full_side * full_side, in_width), jnp.float32)
    empty_carry = jnp.zeros((carry_length,), jnp.float32)
    scalar_zero = jnp.zeros((), jnp.float32)
    empty_stats = (
        jnp.zeros((stat_width,), jnp.float32),
        jnp.zeros((stat_width,), jnp.float32),
        scalar_zero,
    )
    empty_grad_stats = (
        jnp.zeros((stat_width,), jnp.float32),
        jnp.zeros((stat_width,), jnp.float32),
    )
    kept_first = [
        (full_rows, mid_width),
        (mid_width,),
        (),
        (half_rows, mid_width),
        (mid_width,),
        (),
    ]
    kept_second = [
        (half_rows, 2 * out_width),
        (2 * out_width,),
        (),
        (half_rows, mid_width),
        (mid_width,),
        (),
    ]
    kept_third = [(half_rows, mid_width), (mid_width,), ()]
    kept_fourth = [(half_rows, out_width), (out_width,), ()]

    def pack_flat(arrays):
        flat = jnp.concatenate([jnp.reshape(item.astype(jnp.float32), (-1,)) for item in arrays])
        return jnp.pad(flat, (0, carry_length - flat.shape[0]))

    def unpack_flat(flat, shapes):
        result = []
        offset = 0
        for shape_now in shapes:
            count_now = math.prod(shape_now)
            result.append(flat[offset : offset + count_now].reshape(shape_now))
            offset = offset + count_now
        return result

    def gain_of(layer):
        return norm_gains[starts[layer] : starts[layer] + widths[layer]]

    def bias_of(layer):
        return norm_biases[starts[layer] : starts[layer] + widths[layer]]

    def affine(normed, layer):
        return normed * gain_of(layer) + bias_of(layer)

    def add_norm(norm_grads, layer, part):
        return norm_grads.at[starts[layer] : starts[layer] + widths[layer]].add(part)

    def add_parts(weight_grads, layer, upstream, normed):
        gains_grad = add_norm(weight_grads[7], layer, jnp.sum(upstream * normed, axis=0))
        biases_grad = add_norm(weight_grads[8], layer, jnp.sum(upstream, axis=0))
        return weight_grads[:7] + (gains_grad, biases_grad)

    def pad_stat(vector):
        return jnp.pad(vector, (0, stat_width - vector.shape[0]))

    def partial_stats(values, valid_mask):
        masked = values * valid_mask
        return (
            pad_stat(jnp.sum(masked, axis=0)),
            pad_stat(jnp.sum(masked * values, axis=0)),
            jnp.sum(valid_mask),
        )

    def grad_partial(upstream, normed):
        return (pad_stat(jnp.sum(upstream, axis=0)), pad_stat(jnp.sum(upstream * normed, axis=0)))

    def normalize(values, totals):
        total_sum, square_sum, pixel_count = totals
        width_now = values.shape[1]
        channel_mean = total_sum[:width_now] / pixel_count
        inv_std = lax.rsqrt(
            square_sum[:width_now] / pixel_count - channel_mean * channel_mean + EPSILON
        )
        return ((values - channel_mean) * inv_std, inv_std, pixel_count)

    def norm_back(upstream, normed, inv_std, pixel_count, totals, valid_mask, layer):
        bias_total, gain_total = totals
        width_now = upstream.shape[1]
        return (
            gain_of(layer)
            * inv_std
            * (
                upstream
                - bias_total[:width_now] / pixel_count
                - normed * (gain_total[:width_now] / pixel_count)
            )
            * valid_mask
        )

    def stat_sum(parts):
        return lax.psum(parts, "wide")

    def grad_sum(parts):
        return lax.psum(parts, "wide")

    def micro_context(micro_slot):
        full_valid, half_valid = pixel_masks(image_sides[micro_slot], half_side)
        return (full_valid, half_valid, tile_weights(tile_cuts[micro_slot], half_side))

    def masked_inputs(micro_slot, full_valid):
        return jnp.where(
            full_valid > 0,
            inputs[micro_slot].reshape(full_rows, in_width),
            jnp.zeros((), jnp.bfloat16),
        )

    def picked_inputs(micro_slot, full_valid):
        return (
            masked_inputs(micro_slot, full_valid)
            .reshape(images, full_side, full_side, in_width)[:, ::2, ::2, :]
            .reshape(half_rows, in_width)
        )

    def first_columns(normed_one, full_valid):
        active = (smooth(affine(normed_one, 0)) * full_valid).astype(jnp.bfloat16)
        return strided_cols(active.reshape(images, full_side, full_side, mid_width), half_side)

    def second_block(normed_both, half_valid):
        both_out = affine(normed_both, 2)
        branch = both_out[:, :out_width]
        joined = branch + both_out[:, out_width:]
        block_out = smooth(joined) * half_valid
        return (branch, joined, block_out, block_out.astype(jnp.bfloat16))

    def phase_one_first(env, carry, totals, weight_grads):
        full_valid = env[0][0]
        reduced = jnp.dot(
            masked_inputs(env[1], full_valid), w_reduce1, preferred_element_type=jnp.float32
        )
        return (pack_flat([reduced]), partial_stats(reduced, full_valid))

    def phase_one_second(env, carry, totals, weight_grads):
        full_valid, half_valid = (env[0][0], env[0][1])
        expanded = jnp.dot(env[2], w_expand1, preferred_element_type=jnp.float32)
        projected = jnp.dot(
            picked_inputs(env[1], full_valid), w_project1, preferred_element_type=jnp.float32
        )
        both = jnp.concatenate([expanded, projected], axis=1)
        return (pack_flat([both]), partial_stats(both, half_valid))

    def phase_one_third(env, carry, totals, weight_grads):
        half_valid, tap_masks = (env[0][1], env[0][2])
        spatial = jnp.dot(
            tile_cols(env[2], tap_masks, images, half_side),
            second_matrix,
            preferred_element_type=jnp.float32,
        )
        return (pack_flat([spatial]), partial_stats(spatial, half_valid))

    def phase_one_fourth(env, carry, totals, weight_grads):
        expanded = jnp.dot(env[2], w_expand2, preferred_element_type=jnp.float32)
        return (pack_flat([expanded]), partial_stats(expanded, env[0][1]))

    def phase_one_spare(env, carry, totals, weight_grads):
        return (empty_carry, empty_stats)

    def phase_two_first(env, carry, totals, weight_grads):
        full_valid, half_valid = (env[0][0], env[0][1])
        reduced = unpack_flat(carry, [(full_rows, mid_width)])[0]
        normed_one, inv_one, count_one = normalize(reduced, totals)
        spatial = jnp.dot(
            first_columns(normed_one, full_valid), first_matrix, preferred_element_type=jnp.float32
        )
        return (
            pack_flat([normed_one, inv_one, count_one, spatial]),
            partial_stats(spatial, half_valid),
        )

    def phase_two_second(env, carry, totals, weight_grads):
        half_valid = env[0][1]
        both = unpack_flat(carry, [(half_rows, 2 * out_width)])[0]
        normed_one, inv_one, count_one = normalize(both, totals)
        block_low = second_block(normed_one, half_valid)[3]
        reduced = jnp.dot(block_low, w_reduce2, preferred_element_type=jnp.float32)
        return (
            pack_flat([normed_one, inv_one, count_one, reduced]),
            partial_stats(reduced, half_valid),
        )

    def phase_two_third(env, carry, totals, weight_grads):
        spatial = unpack_flat(carry, [(half_rows, mid_width)])[0]
        normed_one, inv_one, count_one = normalize(spatial, totals)
        return (pack_flat([normed_one, inv_one, count_one]), empty_stats)

    def phase_two_fourth(env, carry, totals, weight_grads):
        expanded = unpack_flat(carry, [(half_rows, out_width)])[0]
        normed_one, inv_one, count_one = normalize(expanded, totals)
        return (pack_flat([normed_one, inv_one, count_one]), empty_stats)

    def phase_two_spare(env, carry, totals, weight_grads):
        return (empty_carry, empty_stats)

    def phase_three_first(env, carry, totals, weight_grads):
        half_valid = env[0][1]
        normed_one, inv_one, count_one, spatial = unpack_flat(
            carry, kept_first[:3] + [(half_rows, mid_width)]
        )
        normed_two, inv_two, count_two = normalize(spatial, totals)
        passed = (smooth(affine(normed_two, 1)) * half_valid).astype(jnp.bfloat16)
        return (
            passed,
            empty_out,
            empty_final,
            empty_squares,
            pack_flat([normed_one, inv_one, count_one, normed_two, inv_two, count_two]),
        )

    def phase_three_second(env, carry, totals, weight_grads):
        half_valid = env[0][1]
        normed_one, inv_one, count_one, reduced = unpack_flat(
            carry, kept_second[:3] + [(half_rows, mid_width)]
        )
        branch, joined, block_out, block_low = second_block(normed_one, half_valid)
        normed_two, inv_two, count_two = normalize(reduced, totals)
        passed = (smooth(affine(normed_two, 3)) * half_valid).astype(jnp.bfloat16)
        squares = jnp.stack(
            [
                jnp.sum(branch * branch * half_valid),
                jnp.sum(block_out * block_out),
                scalar_zero,
                scalar_zero,
            ]
        )
        return (
            passed,
            block_low,
            empty_final,
            squares,
            pack_flat([normed_one, inv_one, count_one, normed_two, inv_two, count_two]),
        )

    def phase_three_third(env, carry, totals, weight_grads):
        half_valid = env[0][1]
        normed_one = unpack_flat(carry, kept_third)[0]
        passed = (smooth(affine(normed_one, 4)) * half_valid).astype(jnp.bfloat16)
        return (passed, empty_out, empty_final, empty_squares, carry)

    def phase_three_fourth(env, carry, totals, weight_grads):
        half_valid = env[0][1]
        normed_one = unpack_flat(carry, kept_fourth)[0]
        expanded_out = affine(normed_one, 5)
        joined = expanded_out + env[3].astype(jnp.float32)
        block_out = smooth(joined) * half_valid
        squares = jnp.stack(
            [
                scalar_zero,
                scalar_zero,
                jnp.sum(expanded_out * expanded_out * half_valid),
                jnp.sum(block_out * block_out),
            ]
        )
        return (empty_mid, empty_out, block_out, squares, carry)

    def phase_three_spare(env, carry, totals, weight_grads):
        return (empty_mid, empty_out, empty_final, empty_squares, empty_carry)

    def back_one_first(env, carry, totals, weight_grads):
        half_valid = env[0][1]
        normed_two = unpack_flat(env[6], kept_first)[3]
        upstream = smooth_back(affine(normed_two, 1), env[4].astype(jnp.float32) * half_valid)
        return (pack_flat([upstream]), grad_partial(upstream, normed_two))

    def back_one_second(env, carry, totals, weight_grads):
        half_valid = env[0][1]
        normed_two = unpack_flat(env[6], kept_second)[3]
        upstream = smooth_back(affine(normed_two, 3), env[4].astype(jnp.float32) * half_valid)
        return (pack_flat([upstream]), grad_partial(upstream, normed_two))

    def back_one_third(env, carry, totals, weight_grads):
        half_valid = env[0][1]
        normed_one = unpack_flat(env[6], kept_third)[0]
        upstream = smooth_back(affine(normed_one, 4), env[4].astype(jnp.float32) * half_valid)
        return (pack_flat([upstream]), grad_partial(upstream, normed_one))

    def back_one_fourth(env, carry, totals, weight_grads):
        half_valid = env[0][1]
        normed_one = unpack_flat(env[6], kept_fourth)[0]
        joined = affine(normed_one, 5) + env[3].astype(jnp.float32)
        upstream = cotangent[env[1]].reshape(half_rows, out_width).astype(jnp.float32) * half_valid
        joined_grad = smooth_back(joined, upstream)
        return (pack_flat([joined_grad]), grad_partial(joined_grad, normed_one))

    def back_one_spare(env, carry, totals, weight_grads):
        return (empty_carry, empty_grad_stats)

    def back_two_first(env, carry, totals, weight_grads):
        full_valid, half_valid = (env[0][0], env[0][1])
        normed_one, inv_one, count_one, normed_two, inv_two, count_two = unpack_flat(
            env[6], kept_first
        )
        upstream = unpack_flat(carry, [(half_rows, mid_width)])[0]
        spatial_low = norm_back(
            upstream, normed_two, inv_two, count_two, totals, half_valid, 1
        ).astype(jnp.bfloat16)
        columns = first_columns(normed_one, full_valid)
        weight_grads = replace_at(
            weight_grads,
            1,
            weight_grads[1] + weight_product(columns, spatial_low).reshape(9, mid_width, mid_width),
        )
        weight_grads = add_parts(weight_grads, 1, upstream, normed_two)
        column_grad = jnp.dot(spatial_low, first_matrix.T, preferred_element_type=jnp.float32)
        grid_zero = jnp.zeros((images, full_side, full_side, mid_width), jnp.float32)
        fold_back = jax.vjp(lambda grid_value: strided_cols(grid_value, half_side), grid_zero)[1]
        active_grad = fold_back(column_grad)[0].reshape(full_rows, mid_width)
        upstream_first = smooth_back(affine(normed_one, 0), active_grad * full_valid)
        return (pack_flat([upstream_first]), grad_partial(upstream_first, normed_one), weight_grads)

    def back_two_second(env, carry, totals, weight_grads):
        half_valid = env[0][1]
        normed_one, inv_one, count_one, normed_two, inv_two, count_two = unpack_flat(
            env[6], kept_second
        )
        upstream = unpack_flat(carry, [(half_rows, mid_width)])[0]
        reduced_low = norm_back(
            upstream, normed_two, inv_two, count_two, totals, half_valid, 3
        ).astype(jnp.bfloat16)
        branch, joined, block_out, block_low = second_block(normed_one, half_valid)
        weight_grads = replace_at(
            weight_grads, 4, weight_grads[4] + weight_product(block_low, reduced_low)
        )
        weight_grads = add_parts(weight_grads, 3, upstream, normed_two)
        block_grad = jnp.dot(reduced_low, w_reduce2.T, preferred_element_type=jnp.float32) + env[
            5
        ].astype(jnp.float32)
        joined_grad = smooth_back(joined, block_grad * half_valid)
        both_up = jnp.concatenate([joined_grad, joined_grad], axis=1)
        return (pack_flat([joined_grad]), grad_partial(both_up, normed_one), weight_grads)

    def back_two_third(env, carry, totals, weight_grads):
        half_valid, tap_masks = (env[0][1], env[0][2])
        normed_one, inv_one, count_one = unpack_flat(env[6], kept_third)
        upstream = unpack_flat(carry, [(half_rows, mid_width)])[0]
        spatial_low = norm_back(
            upstream, normed_one, inv_one, count_one, totals, half_valid, 4
        ).astype(jnp.bfloat16)
        columns = tile_cols(env[2], tap_masks, images, half_side)
        weight_grads = replace_at(
            weight_grads,
            5,
            weight_grads[5] + weight_product(columns, spatial_low).reshape(9, mid_width, mid_width),
        )
        weight_grads = add_parts(weight_grads, 4, upstream, normed_one)
        column_grad = jnp.dot(spatial_low, second_matrix.T, preferred_element_type=jnp.float32)
        rows_zero = jnp.zeros((half_rows, mid_width), jnp.float32)
        fold_back = jax.vjp(
            lambda row_value: tile_cols(row_value, tap_masks, images, half_side), rows_zero
        )[1]
        received_grad = fold_back(column_grad)[0]
        return (pack_flat([received_grad]), empty_grad_stats, weight_grads)

    def back_two_fourth(env, carry, totals, weight_grads):
        half_valid = env[0][1]
        normed_one, inv_one, count_one = unpack_flat(env[6], kept_fourth)
        joined_grad = unpack_flat(carry, [(half_rows, out_width)])[0]
        expanded_low = norm_back(
            joined_grad, normed_one, inv_one, count_one, totals, half_valid, 5
        ).astype(jnp.bfloat16)
        weight_grads = replace_at(
            weight_grads, 6, weight_grads[6] + weight_product(env[2], expanded_low)
        )
        weight_grads = add_parts(weight_grads, 5, joined_grad, normed_one)
        received_grad = jnp.dot(expanded_low, w_expand2.T, preferred_element_type=jnp.float32)
        return (pack_flat([received_grad, joined_grad]), empty_grad_stats, weight_grads)

    def back_two_spare(env, carry, totals, weight_grads):
        return (empty_carry, empty_grad_stats, weight_grads)

    def back_three_first(env, carry, totals, weight_grads):
        full_valid = env[0][0]
        normed_one, inv_one, count_one = unpack_flat(env[6], kept_first)[:3]
        upstream = unpack_flat(carry, [(full_rows, mid_width)])[0]
        reduced_low = norm_back(
            upstream, normed_one, inv_one, count_one, totals, full_valid, 0
        ).astype(jnp.bfloat16)
        weight_grads = replace_at(
            weight_grads,
            0,
            weight_grads[0] + weight_product(masked_inputs(env[1], full_valid), reduced_low),
        )
        weight_grads = add_parts(weight_grads, 0, upstream, normed_one)
        input_part = (
            jnp.dot(reduced_low, w_reduce1.T, preferred_element_type=jnp.float32) * full_valid
        ).reshape(images, full_side * full_side, in_width)
        return (empty_mid, empty_out, input_part, weight_grads)

    def back_three_second(env, carry, totals, weight_grads):
        full_valid, half_valid = (env[0][0], env[0][1])
        normed_one, inv_one, count_one = unpack_flat(env[6], kept_second)[:3]
        joined_grad = unpack_flat(carry, [(half_rows, out_width)])[0]
        both_up = jnp.concatenate([joined_grad, joined_grad], axis=1)
        both_low = norm_back(both_up, normed_one, inv_one, count_one, totals, half_valid, 2).astype(
            jnp.bfloat16
        )
        expand_low = both_low[:, :out_width]
        project_low = both_low[:, out_width:]
        weight_grads = replace_at(
            weight_grads, 2, weight_grads[2] + weight_product(env[2], expand_low)
        )
        weight_grads = replace_at(
            weight_grads,
            3,
            weight_grads[3] + weight_product(picked_inputs(env[1], full_valid), project_low),
        )
        weight_grads = add_parts(weight_grads, 2, both_up, normed_one)
        passed_grad = jnp.dot(expand_low, w_expand1.T, preferred_element_type=jnp.float32).astype(
            jnp.bfloat16
        )
        picked_grad = jnp.dot(project_low, w_project1.T, preferred_element_type=jnp.float32)
        grid_grad = (
            jnp.zeros((images, full_side, full_side, in_width), jnp.float32)
            .at[:, ::2, ::2, :]
            .set(picked_grad.reshape(images, half_side, half_side, in_width))
        )
        input_part = (grid_grad.reshape(full_rows, in_width) * full_valid).reshape(
            images, full_side * full_side, in_width
        )
        return (passed_grad, empty_out, input_part, weight_grads)

    def back_three_third(env, carry, totals, weight_grads):
        received_grad = unpack_flat(carry, [(half_rows, mid_width)])[0]
        return (received_grad.astype(jnp.bfloat16), empty_out, empty_input, weight_grads)

    def back_three_fourth(env, carry, totals, weight_grads):
        received_grad, joined_grad = unpack_flat(
            carry, [(half_rows, mid_width), (half_rows, out_width)]
        )
        return (
            received_grad.astype(jnp.bfloat16),
            joined_grad.astype(jnp.bfloat16),
            empty_input,
            weight_grads,
        )

    def back_three_spare(env, carry, totals, weight_grads):
        return (empty_mid, empty_out, empty_input, weight_grads)

    phase_one = [
        phase_one_first,
        phase_one_second,
        phase_one_third,
        phase_one_fourth,
        phase_one_spare,
    ]
    phase_two = [
        phase_two_first,
        phase_two_second,
        phase_two_third,
        phase_two_fourth,
        phase_two_spare,
    ]
    phase_three = [
        phase_three_first,
        phase_three_second,
        phase_three_third,
        phase_three_fourth,
        phase_three_spare,
    ]
    back_one = [back_one_first, back_one_second, back_one_third, back_one_fourth, back_one_spare]
    back_two = [back_two_first, back_two_second, back_two_third, back_two_fourth, back_two_spare]
    back_three = [
        back_three_first,
        back_three_second,
        back_three_third,
        back_three_fourth,
        back_three_spare,
    ]
    weight_grads = (
        jnp.zeros(w_reduce1.shape, jnp.float32),
        jnp.zeros(w_spatial1.shape, jnp.float32),
        jnp.zeros(w_expand1.shape, jnp.float32),
        jnp.zeros(w_project1.shape, jnp.float32),
        jnp.zeros(w_reduce2.shape, jnp.float32),
        jnp.zeros(w_spatial2.shape, jnp.float32),
        jnp.zeros(w_expand2.shape, jnp.float32),
        jnp.zeros(norm_gains.shape, jnp.float32),
        jnp.zeros(norm_biases.shape, jnp.float32),
    )
    msg_store = jnp.zeros((micro_count, half_rows, mid_width), jnp.bfloat16)
    skip_store = jnp.zeros((micro_count, half_rows, out_width), jnp.bfloat16)
    final_store = jnp.zeros((micro_count, half_rows, out_width), jnp.float32)
    kept_store = jnp.zeros((micro_count, carry_length), jnp.float32)
    square_sums = jnp.zeros((4,), jnp.float32)
    for tick_index in range(micro_count + segments - 1):
        current = tick_index - section
        active = (current >= 0) & (current < micro_count)
        micro_slot = jnp.clip(current, 0, micro_count - 1)
        chosen = jnp.where(active, section, 4)
        env = (
            micro_context(micro_slot),
            micro_slot,
            msg_store[micro_slot],
            skip_store[micro_slot],
            empty_mid,
            empty_out,
            empty_carry,
        )
        run_carry, run_parts = lax.switch(
            chosen, phase_one, env, empty_carry, empty_stats, weight_grads
        )
        run_totals = stat_sum(run_parts)
        run_carry, run_parts = lax.switch(
            chosen, phase_two, env, run_carry, run_totals, weight_grads
        )
        run_totals = stat_sum(run_parts)
        msg_out, skip_out, final_out, squares_out, kept_now = lax.switch(
            chosen, phase_three, env, run_carry, run_totals, weight_grads
        )
        kept_store = store_slot(kept_store, kept_now, current, micro_count)
        final_store = final_store.at[micro_slot].add(final_out)
        square_sums = square_sums + squares_out
        relayed = jnp.where(section == 2, skip_store[micro_slot], skip_out)
        bundle = from_behind(shortened(jnp.concatenate([msg_out, relayed], axis=1)), "narrow", 1)
        skip_store = store_slot(
            skip_store, bundle[:, mid_width:], tick_index - section + 1, micro_count
        )
        msg_store = store_slot(
            msg_store, bundle[:, :mid_width], tick_index - section + 1, micro_count
        )
    input_grad = jnp.zeros((micro_count, images, full_side * full_side, in_width), jnp.float32)
    back_store = jnp.zeros((micro_count, half_rows, mid_width), jnp.bfloat16)
    skip_grad_store = jnp.zeros((micro_count, half_rows, out_width), jnp.bfloat16)
    for tick_index in range(micro_count + segments - 1):
        current = tick_index - (segments - 1 - section)
        active = (current >= 0) & (current < micro_count)
        micro_slot = jnp.clip(current, 0, micro_count - 1)
        chosen = jnp.where(active, section, 4)
        context = micro_context(micro_slot)
        env = (
            context,
            micro_slot,
            msg_store[micro_slot],
            skip_store[micro_slot],
            back_store[micro_slot],
            skip_grad_store[micro_slot],
            kept_store[micro_slot],
        )
        carry, parts = lax.switch(
            chosen, back_one, env, empty_carry, empty_grad_stats, weight_grads
        )
        totals = grad_sum(parts)
        carry, parts, weight_grads = lax.switch(chosen, back_two, env, carry, totals, weight_grads)
        totals = grad_sum(parts)
        grad_out, skip_grad_out, input_part, weight_grads = lax.switch(
            chosen, back_three, env, carry, totals, weight_grads
        )
        input_grad = input_grad.at[micro_slot].add(input_part)
        relayed = jnp.where(section == 2, skip_grad_store[micro_slot], skip_grad_out)
        bundle = from_behind(shortened(jnp.concatenate([grad_out, relayed], axis=1)), "narrow", -1)
        skip_grad_store = store_slot(
            skip_grad_store,
            bundle[:, mid_width:],
            tick_index - (segments - 2 - section),
            micro_count,
        )
        back_store = store_slot(
            back_store, bundle[:, :mid_width], tick_index - (segments - 2 - section), micro_count
        )
    out_share, input_share = (
        lax.psum_scatter(
            final_store.reshape(micro_count, images, half_side * half_side, out_width),
            "narrow",
            scatter_dimension=3,
            tiled=True,
        ),
        lax.psum_scatter(input_grad, "narrow", scatter_dimension=3, tiled=True),
    )
    block_output = out_share.astype(jnp.bfloat16)
    input_gradient = input_share.astype(jnp.bfloat16)
    wide_count = lax.axis_size("wide")
    block_count = wide_count * segments
    owned_widths = [
        sum((weight_grads[index].size // block_count for index in owned)) for owned in OWNED_SETS
    ]
    widest = max(owned_widths)

    def packer(owned, width_now):

        def packed():
            joined = jnp.concatenate(
                [block_layout(weight_grads[index], wide_count, segments) for index in owned], axis=2
            )
            padding = jnp.zeros((wide_count, segments, widest - width_now), jnp.float32)
            return jnp.concatenate(
                [
                    joined,
                    padding,
                    weight_grads[7].reshape(wide_count, segments, -1),
                    weight_grads[8].reshape(wide_count, segments, -1),
                ],
                axis=2,
            )

        return packed

    buffer = lax.switch(
        section, [packer(OWNED_SETS[owner], owned_widths[owner]) for owner in range(4)]
    )
    summed = lax.psum_scatter(buffer, "wide", scatter_dimension=0, tiled=True)
    routed = lax.all_to_all(summed, "narrow", split_axis=1, concat_axis=0, tiled=True)
    final_list = [None] * 9
    for owner in range(4):
        offset = 0
        for index in OWNED_SETS[owner]:
            piece_size = weight_grads[index].size // block_count
            final_list[index] = routed[owner, 0, offset : offset + piece_size].reshape(
                shard_shape(weight_grads[index], wide_count, segments)
            )
            offset = offset + piece_size
    norm_piece = weight_grads[7].size // block_count
    final_list[7] = jnp.sum(routed[:, 0, widest : widest + norm_piece], axis=0)
    final_list[8] = jnp.sum(routed[:, 0, widest + norm_piece : widest + 2 * norm_piece], axis=0)
    local_count = jnp.where(
        section == segments - 1,
        jnp.sum((image_sides * image_sides).astype(jnp.float32)),
        scalar_zero,
    )
    square_total, count_total = lax.psum((square_sums, local_count), ("wide", "narrow"))
    rms_values = jnp.sqrt(square_total / (count_total * out_width))
    return (
        block_output,
        input_gradient,
        final_list[0],
        final_list[1],
        final_list[2],
        final_list[3],
        final_list[4],
        final_list[5],
        final_list[6],
        final_list[7],
        final_list[8],
        rms_values,
    )


def solution(mesh):
    return jax.shard_map(
        shards,
        mesh=mesh,
        in_specs=(
            P(None, "wide", None, None),
            P(None, "wide"),
            P(None, "wide", None),
            P(None, "wide", None, None),
            P(),
            P(),
            P(),
            P(),
            P(),
            P(),
            P(),
            P(),
            P(),
        ),
        out_specs=(
            P(None, "wide", None, "narrow"),
            P(None, "wide", None, "narrow"),
            P("wide", "narrow"),
            P(None, "wide", "narrow"),
            P("wide", "narrow"),
            P("wide", "narrow"),
            P("wide", "narrow"),
            P(None, "wide", "narrow"),
            P("wide", "narrow"),
            P(("wide", "narrow")),
            P(("wide", "narrow")),
            P(),
        ),
        check_vma=False,
    )
```

profile of v0, /device:TPU:11, one launch (start us, length us, event | category | flops | bytes accessed | tf_op | source)
XLA Modules:
  0.0 2679.7 jit_solution(3474021574080444123)
XLA Ops:
  18.9 28.3 %all-reduce.387 = (f32[4096]{0:T(1024)S(1)}, f32[]{:T(128)}, f32[4096]{0:T(1024)S(1)}) all-reduce(f32[4096]{0:T(1024)S(1)} %get-tuple-element.5478, f32[]{:T(128)} %get-tuple-element.5479, f32[4096]{0:T(1024)S(1)} %get-tuple-element.5480), channel_id=1, replica_groups=mesh['wide'=8,'narrow'=4] {'wide'}, use_global_device_ids=true, to_apply=%region_18.19 | all-reduce | flops 8193 | bytes 65544 | tf_op jit(solution)/shard_map/psum | solution.py:276
  47.9 27.8 %all-reduce.386 = (f32[4096]{0:T(1024)S(1)}, f32[]{:T(128)}, f32[4096]{0:T(1024)S(1)}) all-reduce(f32[4096]{0:T(1024)S(1)} %get-tuple-element.5482, f32[]{:T(128)} %get-tuple-element.5483, f32[4096]{0:T(1024)S(1)} %get-tuple-element.5484), channel_id=1, replica_groups=mesh['wide'=8,'narrow'=4] {'wide'}, use_global_device_ids=true, to_apply=%region_32.33 | all-reduce | flops 8193 | bytes 65544 | tf_op jit(solution)/shard_map/psum | solution.py:276
  210.3 29.3 %all-reduce.385 = (f32[4096]{0:T(1024)S(1)}, f32[]{:T(128)}, f32[4096]{0:T(1024)S(1)}) all-reduce(f32[4096]{0:T(1024)S(1)} %get-tuple-element.5489, f32[]{:T(128)} %get-tuple-element.5490, f32[4096]{0:T(1024)S(1)} %get-tuple-element.5491), channel_id=1, replica_groups=mesh['wide'=8,'narrow'=4] {'wide'}, use_global_device_ids=true, to_apply=%region_62.63 | all-reduce | flops 8193 | bytes 65544 | tf_op jit(solution)/shard_map/psum | solution.py:276
  243.0 27.5 %all-reduce.384 = (f32[4096]{0:T(1024)S(1)}, f32[]{:T(128)}, f32[4096]{0:T(1024)S(1)}) all-reduce(f32[4096]{0:T(1024)S(1)} %get-tuple-element.5493, f32[]{:T(128)} %get-tuple-element.5494, f32[4096]{0:T(1024)S(1)} %get-tuple-element.5495), channel_id=1, replica_groups=mesh['wide'=8,'narrow'=4] {'wide'}, use_global_device_ids=true, to_apply=%region_76.77 | all-reduce | flops 8193 | bytes 65544 | tf_op jit(solution)/shard_map/psum | solution.py:276
  313.3 29.3 %all-reduce.383 = (f32[4096]{0:T(1024)S(1)}, f32[]{:T(128)}, f32[4096]{0:T(1024)S(1)}) all-reduce(f32[4096]{0:T(1024)S(1)} %get-tuple-element.5500, f32[]{:T(128)} %get-tuple-element.5501, f32[4096]{0:T(1024)S(1)} %get-tuple-element.5502), channel_id=1, replica_groups=mesh['wide'=8,'narrow'=4] {'wide'}, use_global_device_ids=true, to_apply=%region_106.107 | all-reduce | flops 8193 | bytes 65544 | tf_op jit(solution)/shard_map/psum | solution.py:276
  414.7 35.5 %collective-permute-done.2 = bf16[49,2560]{1,0:T(8,128)(2,1)} collective-permute-done((bf16[49,2560]{1,0:T(8,128)(2,1)S(1)}, bf16[49,2560]{1,0:T(8,128)(2,1)}, u32[]{:S(2)}, u32[]{:S(2)}) %collective-permute-start.2) | collective-permute-done | bytes 250912 | tf_op jit(solution)/shard_map/ppermute | solution.py:27
  457.5 29.1 %all-reduce.381 = (f32[4096]{0:T(1024)S(1)}, f32[]{:T(128)}, f32[4096]{0:T(1024)S(1)}) all-reduce(f32[4096]{0:T(1024)S(1)} %get-tuple-element.5511, f32[]{:T(128)} %get-tuple-element.5512, f32[4096]{0:T(1024)S(1)} %get-tuple-element.5513), channel_id=1, replica_groups=mesh['wide'=8,'narrow'=4] {'wide'}, use_global_device_ids=true, to_apply=%region_150.151 | all-reduce | flops 8193 | bytes 65544 | tf_op jit(solution)/shard_map/psum | solution.py:276
  497.8 27.8 %all-reduce.380 = (f32[4096]{0:T(1024)S(1)}, f32[]{:T(128)}, f32[4096]{0:T(1024)S(1)}) all-reduce(f32[4096]{0:T(1024)S(1)} %get-tuple-element.5515, f32[]{:T(128)} %get-tuple-element.5516, f32[4096]{0:T(1024)S(1)} %get-tuple-element.5517), channel_id=1, replica_groups=mesh['wide'=8,'narrow'=4] {'wide'}, use_global_device_ids=true, to_apply=%region_164.165 | all-reduce | flops 8193 | bytes 65544 | tf_op jit(solution)/shard_map/psum | solution.py:276
  573.0 50.2 %collective-permute-done.3 = bf16[49,2560]{1,0:T(8,128)(2,1)} collective-permute-done((bf16[49,2560]{1,0:T(8,128)(2,1)S(1)}, bf16[49,2560]{1,0:T(8,128)(2,1)}, u32[]{:S(2)}, u32[]{:S(2)}) %collective-permute-start.3) | collective-permute-done | bytes 250912 | tf_op jit(solution)/shard_map/ppermute | solution.py:27
  630.5 28.9 %all-reduce.379 = (f32[4096]{0:T(1024)S(1)}, f32[]{:T(128)}, f32[4096]{0:T(1024)S(1)}) all-reduce(f32[4096]{0:T(1024)S(1)} %get-tuple-element.5522, f32[]{:T(128)} %get-tuple-element.5523, f32[4096]{0:T(1024)S(1)} %get-tuple-element.5524), channel_id=1, replica_groups=mesh['wide'=8,'narrow'=4] {'wide'}, use_global_device_ids=true, to_apply=%region_194.195 | all-reduce | flops 8193 | bytes 65544 | tf_op jit(solution)/shard_map/psum | solution.py:276
  670.7 27.9 %all-reduce.378 = (f32[4096]{0:T(1024)S(1)}, f32[]{:T(128)}, f32[4096]{0:T(1024)S(1)}) all-reduce(f32[4096]{0:T(1024)S(1)} %get-tuple-element.5526, f32[]{:T(128)} %get-tuple-element.5527, f32[4096]{0:T(1024)S(1)} %get-tuple-element.5528), channel_id=1, replica_groups=mesh['wide'=8,'narrow'=4] {'wide'}, use_global_device_ids=true, to_apply=%region_208.209 | all-reduce | flops 8193 | bytes 65544 | tf_op jit(solution)/shard_map/psum | solution.py:276
  745.8 50.3 %collective-permute-done.4 = bf16[49,2560]{1,0:T(8,128)(2,1)} collective-permute-done((bf16[49,2560]{1,0:T(8,128)(2,1)S(1)}, bf16[49,2560]{1,0:T(8,128)(2,1)}, u32[]{:S(2)}, u32[]{:S(2)}) %collective-permute-start.4) | collective-permute-done | bytes 250912 | tf_op jit(solution)/shard_map/ppermute | solution.py:27
  803.4 29.6 %all-reduce.377 = (f32[4096]{0:T(1024)S(1)}, f32[]{:T(128)}, f32[4096]{0:T(1024)S(1)}) all-reduce(f32[4096]{0:T(1024)S(1)} %get-tuple-element.5533, f32[]{:T(128)} %get-tuple-element.5534, f32[4096]{0:T(1024)S(1)} %get-tuple-element.5535), channel_id=1, replica_groups=mesh['wide'=8,'narrow'=4] {'wide'}, use_global_device_ids=true, to_apply=%region_238.239 | all-reduce | flops 8193 | bytes 65544 | tf_op jit(solution)/shard_map/psum | solution.py:276
  908.1 31.2 %dynamic-slice_reduce_fusion = (f32[230402]{0:T(1024)}, f32[230402]{0:T(1024)}, f32[230402]{0:T(1024)}, f32[230402]{0:T(1024)}, f32[230402]{0:T(1024)}, /*index=5*/f32[230402]{0:T(1024)}) fusion(f32[3,230402]{1,0:T(4,128)} %dynamic_update_slice.126, s32[]{:T(128)} %min.125, s32[]{:T(128)} %min.122, s32[]{:T(128)} %min.120, s32[]{:T(128)} %min.117, ...), kind=kLoop, calls=%fused_computation.2757 | loop fusion | bytes 11059320 | tf_op jit(solution)/shard_map/dynamic_slice | solution.py:721
  963.2 28.2 %all-reduce.375 = (f32[4096]{0:T(1024)S(1)}, f32[4096]{0:T(1024)S(1)}) all-reduce(f32[4096]{0:T(1024)S(1)} %get-tuple-element.5550, f32[4096]{0:T(1024)S(1)} %get-tuple-element.5551), channel_id=1, replica_groups=mesh['wide'=8,'narrow'=4] {'wide'}, use_global_device_ids=true, to_apply=%region_279.280 | all-reduce | flops 8192 | bytes 65536 | tf_op jit(solution)/shard_map/psum | solution.py:279
  992.9 36.7 %conditional.56 = (f32[230402]{0:T(1024)}, f32[4096]{0:T(1024)S(1)}, f32[4096]{0:T(1024)S(1)}, f32[9,512,512]{2,1,0:T(8,128)}, f32[2048,512]{1,0:T(8,128)}, /*in...) conditional(s32[]{:T(128)} %clamp.32, (f32[8192]{0:T(1024)S(1)}, ...), branch_computations={%region_281.286_spmd, %region_286.291_spmd, %region_291.294_spmd, ... | conditional | flops 470887424 | bytes 68975432 | solution.py:727
  1131.4 32.5 %conditional.59 = (f32[230402]{0:T(1024)}, f32[4096]{0:T(1024)S(1)}, f32[4096]{0:T(1024)S(1)}, f32[9,512,512]{2,1,0:T(8,128)}, f32[2048,512]{1,0:T(8,128)}, /*in...) conditional(s32[]{:T(128)} %clamp.33, (f32[8192]{0:T(1024)S(1)}, ...), branch_computations={%region_326.331_spmd, %region_331.336_spmd, %region_336.339_spmd, ... | conditional | flops 473247744 | bytes 58579712 | solution.py:727
  1268.2 32.6 %conditional.62 = (f32[230402]{0:T(1024)}, f32[4096]{0:T(1024)S(1)}, f32[4096]{0:T(1024)S(1)}, f32[9,512,512]{2,1,0:T(8,128)}, f32[2048,512]{1,0:T(8,128)}, /*in...) conditional(s32[]{:T(128)} %clamp.34, (f32[8192]{0:T(1024)S(1)}, ...), branch_computations={%region_371.376_spmd, %region_376.381_spmd, %region_381.384_spmd, ... | conditional | flops 473247744 | bytes 59927376 | solution.py:727
  1440.7 102.7 %collective-permute-start.9 = (bf16[49,2560]{1,0:T(8,128)(2,1)S(1)}, bf16[49,2560]{1,0:T(8,128)(2,1)}, u32[]{:S(2)}, u32[]{:S(2)}) collective-permute-start(bf16[49,2560]{1,0:T(8,128)(2,1)S(1)} %pad_maximum_fusion.35), channel_id=1, source_target_pairs={{1,0},{2,1},{3,2},{5,4},{6,5},{7,6},{9,8},{10,9},{11,10},{13,12},{... | collective-permute-start | bytes 752648 | tf_op jit(solution)/shard_map/ppermute | solution.py:27
  1624.7 32.5 %collective-permute-start.10 = (bf16[49,2560]{1,0:T(8,128)(2,1)S(1)}, bf16[49,2560]{1,0:T(8,128)(2,1)}, u32[]{:S(2)}, u32[]{:S(2)}) collective-permute-start(bf16[49,2560]{1,0:T(8,128)(2,1)S(1)} %pad_maximum_fusion.36), channel_id=1, source_target_pairs={{1,0},{2,1},{3,2},{5,4},{6,5},{7,6},{9,8},{10,9},{11,10},{13,12},{... | collective-permute-start | bytes 752648 | tf_op jit(solution)/shard_map/ppermute | solution.py:27
  1719.2 58.1 %conditional.73 = (f32[8,4,131584]{2,1,0:T(4,128)}) conditional(s32[]{:T(128)} %clamp.75, (f32[1024,512]{1,0:T(8,128)}, f32[9,512,512]{2,1,0:T(8,128)}, f32[8192]{0:T(1024)S(1)}, f32[8192]{0:T(1024)S(1)}) %tuple.1343, (f32[512,2048]{0,1:T(8,128)}, f32[1024,2048]{1,0:T(8,128)}, f32[2048,512]{1,0:T(8,128)}, ...), branch_computations={%region_536.537_spmd, %region_537.538_spmd, %region_538.539_spmd, ... | conditional | flops 12632064 | bytes 134479872 | solution.py:781
  1749.7 27.6 %pad_maximum_fusion.19 = f32[8,4,131584]{2,1,0:T(4,128)} fusion(f32[8,4,256]{2,1,0:T(4,128)S(1)} %reshape.13348, f32[8,4,256]{2,1,0:T(4,128)S(1)} %reshape.13347, f32[8,4,32768]{2,1,0:T(4,128)} %reshape.13346, f32[131584]{0:T(1024)S(1)} %pad.1494.clone), kind=kLoop, calls=%fused_computation.1821 | loop fusion | flops 12632064 | bytes 21628928 | tf_op jit(solution)/shard_map/cond/branch_3_fun/concatenate | solution.py:769
  1814.1 771.7 %all-reduce.390.cloned.1.call-done = f32[8,4,131584]{2,1,0:T(4,128)} async-done(((f32[8,4,131584]{2,1,0:T(4,128)}), f32[8,4,131584]{2,1,0:T(4,128)}) %all-reduce.390.cloned.1.call-update) | async-done | bytes 16842768
  2600.4 56.6 %all-reduce.363 = (f32[4]{0:T(128)S(1)}, f32[]{:T(128)}) all-reduce(f32[4]{0:T(128)S(1)} %add_add_fusion.6, f32[]{:T(128)S(6)} %select_n.1220), channel_id=1, replica_groups=mesh['wide'=8,'narrow'=4] {'wide','narrow'}, use_global_device_ids=true, to_apply=%region_543.544 | all-reduce | flops 5 | bytes 40 | tf_op jit(solution)/shard_map/psum | solution.py:803
  (919 shorter events, 1352.2 us)
Async XLA Ops:
  8.0 2577.7 %all-reduce.390.cloned.1.call-start = ((), (), s32[]{:S(2)}) async-start(), calls=%async_computation.5 | async-start | bytes 33685504
  16.9 192.1 %copy-start.133 = (f32[196,1]{0,1:T(1,128)}, f32[196,1]{0,1:T(1,128)S(1)}, u32[]{:S(2)}) copy-start(f32[196,1]{0,1:T(1,128)S(1)} %get-tuple-element.7564) | copy-start | bytes 2356
  18.2 221.5 %copy-start.116 = (f32[49,1]{0,1:T(1,128)}, f32[49,1]{0,1:T(1,128)S(1)}, u32[]{:S(2)}) copy-start(f32[49,1]{0,1:T(1,128)S(1)} %get-tuple-element.7570) | copy-start | bytes 592
  77.3 130.7 %collective-permute-start = (bf16[49,2560]{1,0:T(8,128)(2,1)}, bf16[49,2560]{1,0:T(8,128)(2,1)}, u32[]{:S(2)}, u32[]{:S(2)}) collective-permute-start(bf16[49,2560]{1,0:T(8,128)(2,1)} %pad_maximum_fusion.26), channel_id=1, source_target_pairs={{0,1},{1,2},{2,3},{4,5},{5,6},{6,7},{8,9},{9,10},{10,11},{12,13},{... | collective-permute-start | bytes 752648 | tf_op jit(solution)/shard_map/ppermute | solution.py:27
  272.4 37.8 %collective-permute-start.1 = (bf16[49,2560]{1,0:T(8,128)(2,1)S(1)}, bf16[49,2560]{1,0:T(8,128)(2,1)}, u32[]{:S(2)}, u32[]{:S(2)}) collective-permute-start(bf16[49,2560]{1,0:T(8,128)(2,1)S(1)} %pad_maximum_fusion.27), channel_id=1, source_target_pairs={{0,1},{1,2},{2,3},{4,5},{5,6},{6,7},{8,9},{9,10},{10,11},{12,13},{... | collective-permute-start | bytes 752648 | tf_op jit(solution)/shard_map/ppermute | solution.py:27
  376.9 73.3 %collective-permute-start.2 = (bf16[49,2560]{1,0:T(8,128)(2,1)S(1)}, bf16[49,2560]{1,0:T(8,128)(2,1)}, u32[]{:S(2)}, u32[]{:S(2)}) collective-permute-start(bf16[49,2560]{1,0:T(8,128)(2,1)S(1)} %pad_maximum_fusion.28), channel_id=1, source_target_pairs={{0,1},{1,2},{2,3},{4,5},{5,6},{6,7},{8,9},{9,10},{10,11},{12,13},{... | collective-permute-start | bytes 752648 | tf_op jit(solution)/shard_map/ppermute | solution.py:27
  535.0 88.2 %collective-permute-start.3 = (bf16[49,2560]{1,0:T(8,128)(2,1)S(1)}, bf16[49,2560]{1,0:T(8,128)(2,1)}, u32[]{:S(2)}, u32[]{:S(2)}) collective-permute-start(bf16[49,2560]{1,0:T(8,128)(2,1)S(1)} %pad_maximum_fusion.29), channel_id=1, source_target_pairs={{0,1},{1,2},{2,3},{4,5},{5,6},{6,7},{8,9},{9,10},{10,11},{12,13},{... | collective-permute-start | bytes 752648 | tf_op jit(solution)/shard_map/ppermute | solution.py:27
  708.0 88.1 %collective-permute-start.4 = (bf16[49,2560]{1,0:T(8,128)(2,1)S(1)}, bf16[49,2560]{1,0:T(8,128)(2,1)}, u32[]{:S(2)}, u32[]{:S(2)}) collective-permute-start(bf16[49,2560]{1,0:T(8,128)(2,1)S(1)} %pad_maximum_fusion.30), channel_id=1, source_target_pairs={{0,1},{1,2},{2,3},{4,5},{5,6},{6,7},{8,9},{9,10},{10,11},{12,13},{... | collective-permute-start | bytes 752648 | tf_op jit(solution)/shard_map/ppermute | solution.py:27
  906.5 33.9 %collective-permute-start.5 = (bf16[49,2560]{1,0:T(8,128)(2,1)}, bf16[49,2560]{1,0:T(8,128)(2,1)}, u32[]{:S(2)}, u32[]{:S(2)}) collective-permute-start(bf16[49,2560]{1,0:T(8,128)(2,1)} %pad_maximum_fusion.31), channel_id=1, source_target_pairs={{0,1},{1,2},{2,3},{4,5},{5,6},{6,7},{8,9},{9,10},{10,11},{12,13},{... | collective-permute-start | bytes 752648 | tf_op jit(solution)/shard_map/ppermute | solution.py:27
  1071.6 8.8 collective-permute-start.6
  1205.7 10.4 collective-permute-start.7
  1341.3 13.1 collective-permute-start.8
  1429.5 115.2 %copy-start.160 = (pred[49,1,1]{0,1,2:T(4,128)(4,1)S(1)}, pred[49,1,1]{0,1,2:T(4,128)(4,1)}, u32[]{:S(2)}) copy-start(pred[49,1,1]{0,1,2:T(4,128)(4,1)} %get-tuple-element.7439) | copy-start | bytes 151
  1429.5 115.2 %copy-start.161 = (pred[49,1,1]{0,1,2:T(4,128)(4,1)S(1)}, pred[49,1,1]{0,1,2:T(4,128)(4,1)}, u32[]{:S(2)}) copy-start(pred[49,1,1]{0,1,2:T(4,128)(4,1)} %get-tuple-element.7440) | copy-start | bytes 151
  1429.6 115.2 %copy-start.162 = (pred[49,1,1]{0,1,2:T(4,128)(4,1)S(1)}, pred[49,1,1]{0,1,2:T(4,128)(4,1)}, u32[]{:S(2)}) copy-start(pred[49,1,1]{0,1,2:T(4,128)(4,1)} %get-tuple-element.7441) | copy-start | bytes 151
  1429.6 115.2 %copy-start.163 = (pred[49,1,1]{0,1,2:T(4,128)(4,1)S(1)}, pred[49,1,1]{0,1,2:T(4,128)(4,1)}, u32[]{:S(2)}) copy-start(pred[49,1,1]{0,1,2:T(4,128)(4,1)} %get-tuple-element.7442) | copy-start | bytes 151
  1429.6 117.8 %copy-start.186 = (pred[7]{0:T(512)(128)(4,1)S(1)}, pred[7]{0:T(512)(128)(4,1)}, u32[]{:S(2)}) copy-start(pred[7]{0:T(512)(128)(4,1)} %fusion.1302) | copy-start | bytes 25
  1429.6 119.7 %copy-start.184 = (pred[7]{0:T(512)(128)(4,1)S(1)}, pred[7]{0:T(512)(128)(4,1)}, u32[]{:S(2)}) copy-start(pred[7]{0:T(512)(128)(4,1)} %get-tuple-element.7617) | copy-start | bytes 25
  1429.6 120.4 %copy-start.185 = (pred[7]{0:T(512)(128)(4,1)S(1)}, pred[7]{0:T(512)(128)(4,1)}, u32[]{:S(2)}) copy-start(pred[7]{0:T(512)(128)(4,1)} %get-tuple-element.7619) | copy-start | bytes 25
  1440.7 110.0 %collective-permute-start.9 = (bf16[49,2560]{1,0:T(8,128)(2,1)S(1)}, bf16[49,2560]{1,0:T(8,128)(2,1)}, u32[]{:S(2)}, u32[]{:S(2)}) collective-permute-start(bf16[49,2560]{1,0:T(8,128)(2,1)S(1)} %pad_maximum_fusion.35), channel_id=1, source_target_pairs={{1,0},{2,1},{3,2},{5,4},{6,5},{7,6},{9,8},{10,9},{11,10},{13,12},{... | collective-permute-start | bytes 752648 | tf_op jit(solution)/shard_map/ppermute | solution.py:27
  1624.7 33.8 %collective-permute-start.10 = (bf16[49,2560]{1,0:T(8,128)(2,1)S(1)}, bf16[49,2560]{1,0:T(8,128)(2,1)}, u32[]{:S(2)}, u32[]{:S(2)}) collective-permute-start(bf16[49,2560]{1,0:T(8,128)(2,1)S(1)} %pad_maximum_fusion.36), channel_id=1, source_target_pairs={{1,0},{2,1},{3,2},{5,4},{6,5},{7,6},{9,8},{10,9},{11,10},{13,12},{... | collective-permute-start | bytes 752648 | tf_op jit(solution)/shard_map/ppermute | solution.py:27
  1777.3 880.8 %reduce-scatter.3.cloned.1.call-start = ((), (), s32[]{:S(2)}) async-start(), calls=%async_computation.3 | async-start | bytes 1720320 | tf_op jit(solution)/shard_map/reduce_scatter | solution.py:745
  1791.2 868.6 %reduce-scatter.5.cloned.1.call-start = ((), (), s32[]{:S(2)}) async-start(), calls=%async_computation.4 | async-start | bytes 3072000 | tf_op jit(solution)/shard_map/reduce_scatter | solution.py:751
  2593.3 68.3 %all-to-all-start = ((f32[1,4,131584]{2,0,1:T(1,128)}), f32[1,4,131584]{2,0,1:T(1,128)}, u32[]{:S(2)}, u32[]{:S(2)}) async-start(f32[1,4,131584]{2,0,1:T(1,128)} %copy.442), calls=%async_computation.2 | async-start | bytes 4210688 | tf_op jit(solution)/shard_map/all_to_all | solution.py:785
  (87 other events, 3429.6 us)
Sparse Core Ops, SparseCore 0:
  1777.4 808.2 all-reduce.389
Sparse Core Ops, SparseCore 1:
  1791.3 323.8 reduce-scatter.2
  2117.8 33.6 reduce-scatter.4
where the time goes:
time: 2710 us; the launch traced here: 2680 us
  waiting for transfers between devices  909 us (34%)
  blocking collectives  715 us (26%)
  local copies, waits for them, and re-layouts  537 us (20%)
  other arithmetic  227 us (8%)
  starting transfers between devices  173 us (6%)
  loops' own time  70.8 us (3%)
    unnamed x4, waiting for transfers between devices  772 us
    psum x12, blocking collectives, stat_sum(): return lax.psum(parts, 'wide')  340 us
    psum x12, blocking collectives, grad_sum(): return lax.psum(parts, 'wide')  318 us
    ppermute x11, starting transfers between devices, from_behind(): return lax.ppermute(shard, axis, pairs)  167 us
    ppermute x11, waiting for transfers between devices, from_behind(): return lax.ppermute(shard, axis, pairs)  137 us
    dynamic_update_slice x6, local copies, waits for them, and re-layouts, store_slot(): lax.dynamic_update_index_in_dim(store, jnp.where(inside, value, store[pla...  107 us
    dynamic_slice x21, local copies, waits for them, and re-layouts, store_slot(): store[place_at]  70.5 us
    another operation x93, local copies, waits for them, and re-layouts  58.3 us
  transfers between devices with their start and end apart: 15, of which 5 were waited for; matrix products, arithmetic and copies ran while one was open for 14% of the time, Pallas kernels for 0%

commit v1 on v0

v1 whole, which is shorter than its diff:
```python
import functools
import math
from types import SimpleNamespace

import jax
import jax.numpy as jnp
from jax import lax
from jax.experimental import pallas as pl
from jax.experimental.pallas import tpu as pltpu
from jax.sharding import PartitionSpec as P

MESH = pl.DeviceIdType.MESH
WIDE, NARROW = "wide", "narrow"
BF16 = jnp.bfloat16
F32 = jnp.float32
HALF = 7
FULL = 2 * HALF
EPSILON = 1e-05
C0 = math.sqrt(2.0 / math.pi)
C1 = C0 * 0.044715
HR = 64
FR = 208
TAPS = 9


def dot(a, b):
    return jnp.dot(a, b, preferred_element_type=F32)


def dot_nt(a, b):
    return lax.dot_general(a, b, (((1,), (1,)), ((), ())), preferred_element_type=F32)


def dot_tn(a, b):
    return lax.dot_general(a, b, (((0,), (0,)), ((), ())), preferred_element_type=F32)


def spread(mask, width):
    return jnp.concatenate([mask] * (width // 128), axis=1)


def gelu(v):
    t = jnp.tanh(v * (C0 + C1 * (v * v)))
    h = 0.5 * v
    return h + h * t


def gelu_slope(v):
    v2 = v * v
    t = jnp.tanh(v * (C0 + C1 * v2))
    return 0.5 + 0.5 * t + (0.5 * v) * (1.0 - t * t) * (C0 + (3.0 * C1) * v2)


def column_sum(values):
    return jnp.sum(values, axis=0, keepdims=True)


def half_cell(p):
    i = lax.shift_right_logical(p * 9363, 16)
    return i, p - HALF * i


def full_cell(p):
    i = lax.shift_right_logical(p * 4682, 16)
    return i, p - FULL * i


def tap_of(r):
    t = lax.shift_right_logical(r, 6)
    ta = lax.shift_right_logical(t * 11, 5)
    return ta - 1, t - 3 * ta - 1


def one_zero(condition):
    return jnp.where(condition, 1.0, 0.0)


def strided_pick(rows, cells):
    a, b = tap_of(rows)
    p = lax.bitwise_and(rows, 63)
    i, j = half_cell(p)
    r, c = 2 * i + a, 2 * j + b
    inside = (p < HALF * HALF) & (r >= 0) & (r < FULL) & (c >= 0) & (c < FULL)
    return one_zero(inside & (cells == r * FULL + c)).astype(BF16)


def tile_pick(rows, cells, cut_row, cut_col):
    a, b = tap_of(rows)
    p = lax.bitwise_and(rows, 63)
    i, j = half_cell(p)
    r, c = i + a, j + b
    inside = (p < HALF * HALF) & (r >= 0) & (r < HALF) & (c >= 0) & (c < HALF)
    row_far = one_zero(r >= cut_row) - one_zero(i >= cut_row)
    col_far = one_zero(c >= cut_col) - one_zero(j >= cut_col)
    same = (row_far == 0.0) & (col_far == 0.0)
    return one_zero(inside & same & (cells == r * HALF + c)).astype(BF16)


class Group:
    def __init__(self, sems):
        self.sems = sems
        self.used = 0
        self.items = []

    def sem(self):
        self.used += 1
        return self.sems.at[self.used - 1]

    def remote(self, src, dst, recv_sem, device, when=None):
        copy = pltpu.make_async_remote_copy(
            src_ref=src, dst_ref=dst, send_sem=self.sem(), recv_sem=recv_sem,
            device_id=device, device_id_type=MESH,
        )
        if when is None:
            copy.start()
        else:
            pl.when(when)(copy.start)
        self.items.append((copy, when))

    def finish(self):
        for copy, when in self.items:
            if when is None:
                copy.wait_send()
            else:
                pl.when(when)(copy.wait_send)


def wait_bytes(ref, sem):
    pltpu.make_async_copy(ref, ref, sem).wait()


def kernel(plan, *refs):
    r = SimpleNamespace(**dict(zip(plan.names, refs)))
    r.stat = [getattr(r, "stat%d" % step) for step in range(12)]
    wide, narrow, micros, slots = plan.wide, plan.narrow, plan.micros, plan.slots
    mid, out, inw, allch = plan.mid, plan.out, plan.inw, plan.allch
    pairs = wide // 2
    columns = narrow // 2
    starts, layers = plan.starts, plan.layers
    w = lax.axis_index(WIDE)
    n = lax.axis_index(NARROW)
    x = n // 2
    core = n % 2
    first_micro = x * slots
    fetch = r.fetch

    def micro_of(s):
        return lax.rem(first_micro + s, micros)

    barrier = pltpu.get_barrier_semaphore()

    @pl.loop(1, wide)
    def _(d):
        pl.semaphore_signal(
            barrier, inc=1, device_id=(lax.rem(w + d, wide), n), device_id_type=MESH
        )

    for d in range(1, narrow):
        pl.semaphore_signal(
            barrier, inc=1, device_id=(w, lax.rem(n + d, narrow)), device_id_type=MESH
        )

    def pass_barrier():
        pl.semaphore_wait(barrier, wide - 1 + narrow - 1)

    def build_picks():
        rows = lax.broadcasted_iota(jnp.int32, (TAPS * HR, FR), 0)
        cells = lax.broadcasted_iota(jnp.int32, (TAPS * HR, FR), 1)
        r.pick[...] = strided_pick(rows, cells)

    def build_pick_back():
        rows = lax.broadcasted_iota(jnp.int32, (FR, TAPS * HR), 1)
        cells = lax.broadcasted_iota(jnp.int32, (FR, TAPS * HR), 0)
        r.pick_back[...] = strided_pick(rows, cells)

    def build_tiles(slot, micro):
        rows = lax.broadcasted_iota(jnp.int32, (TAPS * HR, HR), 0)
        cells = lax.broadcasted_iota(jnp.int32, (TAPS * HR, HR), 1)
        r.tiles[slot] = tile_pick(
            rows, cells, r.tile_cuts[0, 0, micro], r.tile_cuts[0, 1, micro]
        )

    def full_mask(micro):
        row, col = full_cell(lax.broadcasted_iota(jnp.int32, (FR, 128), 0))
        limit = 2 * r.image_sides[0, micro]
        return one_zero((row < limit) & (col < limit))

    def half_mask(micro):
        row, col = half_cell(lax.broadcasted_iota(jnp.int32, (HR, 128), 0))
        limit = r.image_sides[0, micro]
        return one_zero((row < limit) & (col < limit))

    def fetch_image(slot, micro):
        return pltpu.make_async_copy(r.inputs.at[micro, 0], r.raw.at[slot], fetch.at[slot])

    def mask_image(slot, micro):
        mask = full_mask(micro)
        raw = jnp.concatenate(
            [r.raw[slot].astype(F32), jnp.zeros((FR - FULL * FULL, inw), F32)], axis=0
        )
        r.image[slot] = (raw * spread(mask, inw)).astype(BF16)

    def chain(*local):
        r.__dict__.update(zip(plan.chain_names, local))
        group = Group(r.chain_sends)
        weights = (
            (r.w_reduce1, r.k_reduce1), (r.w_spatial1, r.k_spatial1), (r.w_project1, r.k_project1),
            (r.w_expand1, r.k_expand1), (r.w_reduce2, r.k_reduce2), (r.w_spatial2, r.k_spatial2),
            (r.w_expand2, r.k_expand2),
        )

        def fetch_weight(index):
            return pltpu.make_async_copy(*weights[index], fetch.at[4 + index])

        fetch_image(0, micro_of(0)).start()
        fetch_weight(0).start()
        for s in range(1, slots):
            fetch_image(s, micro_of(s)).start()
        for index in range(1, 7):
            fetch_weight(index).start()

        def fetch_cotangent(s):
            return pltpu.make_async_copy(
                r.cotangent.at[micro_of(s), 0], r.cot_raw.at[s], fetch.at[11 + s]
            )

        for s in range(slots):
            fetch_cotangent(s).start()
            r.half[s] = half_mask(micro_of(s))
            r.full[s] = full_mask(micro_of(s))

        def send_stats(step):
            stat = r.stat[step]

            @pl.loop(0, wide)
            def _(d):
                p = lax.rem(wide - 1 - w + d, wide)

                @pl.when(p != w)
                def _():
                    pltpu.make_async_remote_copy(
                        src_ref=stat.at[w], dst_ref=stat.at[w],
                        send_sem=r.stat_send.at[step], recv_sem=r.stat_recv.at[step],
                        device_id=(p, n), device_id_type=MESH,
                    ).start()

        def wait_stats(step):
            stat = r.stat[step]
            wait_bytes(stat.at[pl.ds(0, wide - 1)], r.stat_recv.at[step])

        def total(step, row, begin=0, width=None):
            stat = r.stat[step]
            width = stat.shape[2] if width is None else width
            part = stat[0, row : row + 1, begin : begin + width]
            for j in range(1, wide):
                part = part + stat[j, row : row + 1, begin : begin + width]
            return part

        def put(step, row, value, begin=0):
            r.stat[step][w, row : row + 1, begin : begin + value.shape[1]] = value

        def put_pair(step, s, values, begin=0):
            put(step, 2 * s, column_sum(values), begin)
            put(step, 2 * s + 1, column_sum(values * values), begin)

        def inverse_count(s, layer):
            count = r.counts[s : s + 1, 0:1]
            return 1.0 / (count * (4.0 if layer == 0 else 1.0))

        def settle(s, layer, step, begin=0):
            start, width = layers[layer]
            inv_n = inverse_count(s, layer)
            mean = total(step, 2 * s, begin, width) * inv_n
            square = total(step, 2 * s + 1, begin, width) * inv_n
            inv = lax.rsqrt(square - mean * mean + EPSILON)
            scale = r.gains[:, start : start + width] * inv
            r.norms[2 * s : 2 * s + 1, start : start + width] = inv
            r.norms[2 * s + 1 : 2 * s + 2, start : start + width] = -mean * inv
            return scale, r.biases[:, start : start + width] - mean * scale

        def kept(s, layer):
            start, width = layers[layer]
            gain = r.gains[:, start : start + width]
            inv = r.norms[2 * s : 2 * s + 1, start : start + width]
            offset = r.norms[2 * s + 1 : 2 * s + 2, start : start + width]
            return inv, offset, gain * inv, r.biases[:, start : start + width] + gain * offset

        def normed(s, layer, z):
            inv, offset, _, _ = kept(s, layer)
            return z * inv + offset

        def activation(s, layer, z):
            _, _, scale, shift = kept(s, layer)
            return z * scale + shift

        def settle_back(s, layer, step, sum_row, gain_row, begin=0):
            start, width = layers[layer]
            sum_u = total(step, sum_row, begin, width)
            sum_g = total(step, gain_row, begin, width)
            live = jnp.where(first_micro + s < micros, 1.0, 0.0)
            for row, value in ((0, sum_g), (1, sum_u)):
                if s == 0:
                    r.norm_sums[row : row + 1, start : start + width] = value
                else:
                    r.norm_sums[row : row + 1, start : start + width] += live * value
            inv_n = inverse_count(s, layer)
            inv, offset, k0, _ = kept(s, layer)
            k2 = -k0 * (sum_g * inv_n)
            return k0, -k0 * (sum_u * inv_n) + k2 * offset, k2 * inv

        def live_row(s, row):
            if s == 0:
                return row
            return row * jnp.where(first_micro + s < micros, 1.0, 0.0)

        def fold_row(row):
            parts = [row[:, c : c + mid] for c in range(0, row.shape[1], mid)]
            return functools.reduce(lambda a, b: a + b, parts)

        def add_squares(s, index, values):
            row = live_row(s, fold_row(column_sum(values)))
            if s == 0:
                r.squares[index : index + 1, :] = row
            else:
                r.squares[index : index + 1, :] += row

        def share(src, dst, recv_sem, cut=None):
            for c in range(columns):
                amount = min(slots, micros - c * slots)
                if amount <= 0:
                    continue
                for h in range(columns):
                    part = src.at[0:amount]
                    if cut is not None:
                        part = src.at[0:amount, :, h * cut : (h + 1) * cut]
                    group.remote(
                        part, dst.at[c * slots : c * slots + amount], recv_sem,
                        (w, 2 * h), x == c,
                    )

        def rows2(ref):
            value = ref[...]
            return value.reshape(value.shape[0] * value.shape[1], value.shape[2])

        def set_rows(ref, value):
            ref[...] = value.reshape(ref.shape)

        def rows_of(value, s, count=HR):
            return value[s * count : (s + 1) * count]

        def gather_tiles(s, value, select):
            picked = dot(select, value).astype(BF16)
            for t in range(TAPS):
                r.cols[s * HR : (s + 1) * HR, t * mid : (t + 1) * mid] = picked[
                    t * HR : (t + 1) * HR
                ]

        def half_wide(s, width):
            return spread(r.half[s], width)

        for s in range(slots):
            fetch_image(s, micro_of(s)).wait()
            mask_image(s, micro_of(s))
        fetch_weight(0).wait()
        for s in range(slots):
            z = dot(r.image[s], r.k_reduce1[...])
            r.z0[s] = z
            put_pair(0, s, z)
            side = r.image_sides[0, micro_of(s)]
            area = jnp.full((1, mid), side * side, jnp.int32).astype(F32)
            put(0, 2 * slots + s, area)
        pass_barrier()
        send_stats(0)
        build_picks()
        for s in range(slots):
            build_tiles(s, micro_of(s))
        centre = r.pick[4 * HR : 5 * HR, :]
        for s in range(slots):
            r.picked[s * HR : (s + 1) * HR, :] = dot(centre, r.image[s]).astype(BF16)
        fetch_weight(2).wait()
        set_rows(r.z_short, dot(r.picked[...], r.k_project1[...]))
        for s in range(slots):
            put_pair(2, s, r.z_short[s], out)
        fetch_weight(1).wait()
        wait_stats(0)
        for s in range(slots):
            r.counts[s : s + 1, :] = total(0, 2 * slots + s, 0, 128)

        for s in range(slots):
            scale, shift = settle(s, 0, 0)
            act = gelu(r.z0[s] * scale + shift) * spread(r.full[s], mid)
            act = act.astype(BF16)
            r.act1[s] = act
            gather_tiles(s, act, r.pick[...])
        z = dot(r.cols[...], r.k_spatial1[...])
        for s in range(slots):
            r.z1[s] = rows_of(z, s)
            put_pair(1, s, rows_of(z, s) * half_wide(s, mid))
        send_stats(1)
        share(r.act1, r.h_act1, r.h_recv.at[0])
        for s in range(slots):
            r.slope0[s] = gelu_slope(activation(s, 0, r.z0[s])) * spread(r.full[s], mid)
        fetch_weight(3).wait()
        wait_stats(1)

        for s in range(slots):
            scale, shift = settle(s, 1, 1)
            mixed = gelu(r.z1[s] * scale + shift) * half_wide(s, mid)
            r.mix1[s] = mixed.astype(BF16)
        z = dot(rows2(r.mix1), r.k_expand1[...])
        for s in range(slots):
            r.z_branch[s] = rows_of(z, s)
            put_pair(2, s, rows_of(z, s))
        send_stats(2)
        share(r.mix1, r.h_mix1, r.h_recv.at[1])
        for s in range(slots):
            r.slope1[s] = gelu_slope(activation(s, 1, r.z1[s])) * half_wide(s, mid)
        fetch_weight(4).wait()
        wait_stats(2)

        for s in range(slots):
            scale, shift = settle(s, 2, 2, 0)
            scale_short, shift_short = settle(s, 3, 2, out)
            joined = (r.z_branch[s] * scale + shift) + (
                r.z_short[s] * scale_short + shift_short
            )
            r.slope2[s] = joined
            block = gelu(joined) * half_wide(s, out)
            r.low1[s] = block.astype(BF16)
        z = dot(rows2(r.low1), r.k_reduce2[...])
        for s in range(slots):
            r.z3[s] = rows_of(z, s)
            put_pair(3, s, rows_of(z, s))
        send_stats(3)
        share(r.low1, r.h_low1, r.h_recv.at[2])
        for s in range(slots):
            mask = half_wide(s, out)
            branch = activation(s, 2, r.z_branch[s])
            joined = r.slope2[s]
            add_squares(s, 0, branch * branch * mask)
            block = gelu(joined) * mask
            add_squares(s, 1, block * block)
            r.slope2[s] = gelu_slope(joined) * mask
        fetch_weight(5).wait()
        wait_stats(3)

        for s in range(slots):
            scale, shift = settle(s, 4, 3)
            act = gelu(r.z3[s] * scale + shift) * half_wide(s, mid)
            act = act.astype(BF16)
            r.act2[s] = act
            gather_tiles(s, act, r.tiles[s])
        z = dot(r.cols[...], r.k_spatial2[...])
        for s in range(slots):
            r.z4[s] = rows_of(z, s)
            put_pair(4, s, rows_of(z, s) * half_wide(s, mid))
        send_stats(4)
        share(r.act2, r.h_act2, r.h_recv.at[3])
        for s in range(slots):
            r.slope3[s] = gelu_slope(activation(s, 4, r.z3[s])) * half_wide(s, mid)
        fetch_weight(6).wait()
        wait_stats(4)

        for s in range(slots):
            scale, shift = settle(s, 5, 4)
            mixed = gelu(r.z4[s] * scale + shift) * half_wide(s, mid)
            r.mix2[s] = mixed.astype(BF16)
        z = dot(rows2(r.mix2), r.k_expand2[...])
        for s in range(slots):
            r.z5[s] = rows_of(z, s)
            put_pair(5, s, rows_of(z, s))
        send_stats(5)
        share(r.mix2, r.h_mix2, r.h_recv.at[4])
        for s in range(slots):
            r.slope4[s] = gelu_slope(activation(s, 5, r.z4[s])) * half_wide(s, mid)
            fetch_cotangent(s).wait()
        wait_stats(5)

        for s in range(slots):
            scale, shift = settle(s, 6, 5)
            joined = (r.z5[s] * scale + shift) + r.low1[s].astype(F32)
            cot = jnp.concatenate(
                [r.cot_raw[s].astype(F32), jnp.zeros((HR - HALF * HALF, out), F32)], axis=0
            )
            u = gelu_slope(joined) * cot * half_wide(s, out)
            r.u_out[s] = u
            put(6, 2 * s, column_sum(u))
            put(6, 2 * s + 1, column_sum(u * normed(s, 6, r.z5[s])))
        send_stats(6)
        for s in range(slots):
            mask = half_wide(s, out)
            branch = activation(s, 6, r.z5[s])
            add_squares(s, 2, branch * branch * mask)
            block = gelu(branch + r.low1[s].astype(F32)) * mask
            add_squares(s, 3, block * block)
            r.final[s] = block.astype(BF16)
        part = out // narrow
        for s in range(slots):
            for target in range(narrow):
                src = r.final.at[s, :, target * part : (target + 1) * part]
                dst = r.o_final.at[first_micro + s]
                group.remote(
                    src, dst, r.o_recv.at[0], (w, target),
                    (first_micro + s < micros) & (n != target),
                )
        for index in range(4):
            put(7, 2 * slots + index, r.squares[index : index + 1, :])
        wait_stats(6)

        for s in range(slots):
            k0, k1, k2 = settle_back(s, 6, 6, 2 * s, 2 * s + 1)
            grad = (k0 * r.u_out[s] + k1 + k2 * r.z5[s]) * half_wide(s, out)
            r.g_e2[s] = grad.astype(BF16)
        back = dot_nt(rows2(r.g_e2), r.k_expand2[...]).astype(BF16).astype(F32)
        for s in range(slots):
            u = rows_of(back, s) * r.slope4[s]
            r.u_mid[s] = u
            put(7, 2 * s, column_sum(u))
            put(7, 2 * s + 1, column_sum(u * normed(s, 5, r.z4[s])))
        send_stats(7)
        share(r.g_e2, r.h_g_e2, r.h_recv.at[5], out // columns)
        wait_stats(7)
        for index in range(4):
            r.rms_part[index : index + 1, :] = total(7, 2 * slots + index)
        count = r.counts[0:1, :]
        for s in range(1, slots):
            count = count + live_row(s, r.counts[s : s + 1, :])
        r.rms_part[4:5, :] = spread(count, mid)

        for s in range(slots):
            k0, k1, k2 = settle_back(s, 5, 7, 2 * s, 2 * s + 1)
            grad = (k0 * r.u_mid[s] + k1 + k2 * r.z4[s]) * half_wide(s, mid)
            r.g_s2[s] = grad.astype(BF16)
            gather_tiles(s, r.g_s2[s], r.tiles[s])
        back = None
        for t in range(TAPS):
            back_tap = dot_nt(
                r.cols[:, t * mid : (t + 1) * mid],
                r.k_spatial2[(8 - t) * mid : (9 - t) * mid, :],
            )
            back = back_tap if back is None else back + back_tap
        back = back.astype(BF16).astype(F32)
        for s in range(slots):
            u = rows_of(back, s) * r.slope3[s]
            r.u_mid[s] = u
            put(8, 2 * s, column_sum(u))
            put(8, 2 * s + 1, column_sum(u * normed(s, 4, r.z3[s])))
        send_stats(8)
        share(r.g_s2, r.h_g_s2, r.h_recv.at[6], mid // columns)
        wait_stats(8)

        for s in range(slots):
            k0, k1, k2 = settle_back(s, 4, 8, 2 * s, 2 * s + 1)
            grad = (k0 * r.u_mid[s] + k1 + k2 * r.z3[s]) * half_wide(s, mid)
            r.g_r2[s] = grad.astype(BF16)
        back = dot_nt(rows2(r.g_r2), r.k_reduce2[...])
        for s in range(slots):
            u = (rows_of(back, s) + r.u_out[s].astype(BF16).astype(F32)) * r.slope2[s]
            r.u_out[s] = u
            put(9, 3 * s, column_sum(u))
            put(9, 3 * s + 1, column_sum(u * normed(s, 2, r.z_branch[s])))
            put(9, 3 * s + 2, column_sum(u * normed(s, 3, r.z_short[s])))
        send_stats(9)
        share(r.g_r2, r.h_g_r2, r.h_recv.at[7], mid // columns)
        wait_stats(9)

        for s in range(slots):
            k0, k1, k2 = settle_back(s, 2, 9, 3 * s, 3 * s + 1)
            grad = (k0 * r.u_out[s] + k1 + k2 * r.z_branch[s]) * half_wide(s, out)
            r.g_e1[s] = grad.astype(BF16)
        back = dot_nt(rows2(r.g_e1), r.k_expand1[...]).astype(BF16).astype(F32)
        for s in range(slots):
            u = rows_of(back, s) * r.slope1[s]
            r.u_mid[s] = u
            put(10, 2 * s, column_sum(u))
            put(10, 2 * s + 1, column_sum(u * normed(s, 1, r.z1[s])))
        send_stats(10)
        share(r.g_e1, r.h_g_e1, r.h_recv.at[8], out // columns)
        for s in range(slots):
            k0, k1, k2 = settle_back(s, 3, 9, 3 * s, 3 * s + 2)
            grad = (k0 * r.u_out[s] + k1 + k2 * r.z_short[s]) * half_wide(s, out)
            r.g_p1[s] = grad.astype(BF16)
        share(r.g_p1, r.h_g_p1, r.h_recv.at[9], out // columns)
        build_pick_back()
        r.picked[...] = dot_nt(rows2(r.g_p1), r.k_project1[...]).astype(
            BF16
        )
        wait_stats(10)

        for s in range(slots):
            k0, k1, k2 = settle_back(s, 1, 10, 2 * s, 2 * s + 1)
            grad = (k0 * r.u_mid[s] + k1 + k2 * r.z1[s]) * half_wide(s, mid)
            r.g_s1[s] = grad.astype(BF16)
        g_rows = rows2(r.g_s1)
        for t in range(TAPS):
            r.cols[:, t * mid : (t + 1) * mid] = dot_nt(
                g_rows, r.k_spatial1[t * mid : (t + 1) * mid, :]
            ).astype(BF16)
        for s in range(slots):
            back = jnp.concatenate(
                [r.cols[s * HR : (s + 1) * HR, t * mid : (t + 1) * mid] for t in range(TAPS)],
                axis=0,
            )
            u = dot(r.pick_back[...], back) * r.slope0[s]
            r.slope0[s] = u
            put(11, 2 * s, column_sum(u))
            put(11, 2 * s + 1, column_sum(u * normed(s, 0, r.z0[s])))
        send_stats(11)
        share(r.g_s1, r.h_g_s1, r.h_recv.at[10], mid // columns)
        wait_stats(11)

        for s in range(slots):
            k0, k1, k2 = settle_back(s, 0, 11, 2 * s, 2 * s + 1)
            grad = (k0 * r.slope0[s] + k1 + k2 * r.z0[s]) * spread(r.full[s], mid)
            r.g_r1[s] = grad.astype(BF16)
        share(r.g_r1, r.h_g_r1, r.h_recv.at[11], mid // columns)
        section = allch // wide
        own = pl.ds(pl.multiple_of(w * section, 128), section)
        for target in range(narrow):
            group.remote(
                r.norm_sums.at[:, own], r.o_norms.at[x], r.o_recv.at[2], (w, target),
                n != target,
            )
            group.remote(
                r.rms_part, r.o_rms.at[x], r.o_recv.at[3], (w, target), n != target
            )
        r.o_norms[x] = r.norm_sums[:, own]
        r.o_rms[x] = r.rms_part[...]
        for s in range(slots):
            grad = dot_nt(r.g_r1[s], r.k_reduce1[...])
            grad = grad + dot(
                r.pick_back[:, 4 * HR : 5 * HR], r.picked[s * HR : (s + 1) * HR, :]
            )
            r.image[s] = grad.astype(BF16)
        part = inw // narrow
        for s in range(slots):
            for target in range(narrow):
                group.remote(
                    r.image.at[s, :, target * part : (target + 1) * part],
                    r.o_input.at[first_micro + s], r.o_recv.at[1], (w, target),
                    (first_micro + s < micros) & (n != target),
                )
        for s in range(slots):
            for target in range(narrow):

                @pl.when((n == target) & (first_micro + s < micros))
                def _(s=s, target=target):
                    wide_part = out // narrow
                    r.o_final[first_micro + s] = r.final[
                        s, :, target * wide_part : (target + 1) * wide_part
                    ]
                    r.o_input[first_micro + s] = r.image[
                        s, :, target * part : (target + 1) * part
                    ]

        for c in range(columns):
            amount = min(slots, micros - c * slots)
            others = micros - max(amount, 0)

            @pl.when(x == c)
            def _(others=others):
                wait_bytes(r.o_final.at[0:others], r.o_recv.at[0])
                wait_bytes(r.o_input.at[0:others], r.o_recv.at[1])

        wait_bytes(r.o_norms.at[0 : columns - 1], r.o_recv.at[2])
        wait_bytes(r.o_rms.at[0 : columns - 1], r.o_recv.at[3])
        for index, spec in enumerate(plan.products):
            wait_bytes(getattr(r, "out_" + spec.name), r.w_recv.at[index])
        group.finish()
        for step in range(12):
            wait_bytes(r.stat[step].at[pl.ds(0, wide - 1)], r.stat_send.at[step])

    def helper(*local):
        r.__dict__.update(zip(plan.helper_names, local))
        group = Group(r.helper_sends)
        parity = w % 2
        place = w // 2
        partner = w + 1 - 2 * parity

        for m in range(micros):
            fetch_image(m, m).start()
        build_picks()
        for m in range(micros):
            build_tiles(m, m)
        for m in range(micros):
            fetch_image(m, m).wait()
            mask_image(m, m)
        centre = r.pick[4 * HR : 5 * HR, :]
        for m in range(micros):
            r.picked[m * HR : (m + 1) * HR, :] = dot(centre, r.image[m]).astype(BF16)
        pass_barrier()

        def tall(ref):
            value = ref[...]
            return value.reshape(value.shape[0] * value.shape[1], value.shape[2])

        def multiply(spec):
            name, rows = spec.name, spec.rows
            grad = tall(getattr(r, "h_g_" + name))
            product = getattr(r, "p_" + name)
            if spec.taps == 1:
                left = r.picked if name == "p1" else None
                chunk = min(256, spec.depth)
                for begin in range(0, spec.depth, chunk):
                    if name == "p1":
                        piece = left[:, begin : begin + chunk]
                    else:
                        source = getattr(r, spec.left)
                        piece = source[:, :, begin : begin + chunk]
                        piece = piece.reshape(piece.shape[0] * piece.shape[1], chunk)
                    value = dot_tn(piece, grad).astype(BF16)
                    for b in range(chunk // rows):
                        block = begin // rows + b
                        product[block // 2, block % 2, 0] = value[b * rows : (b + 1) * rows]
            else:
                for m in range(micros):
                    select = r.pick[...] if name == "s1" else r.tiles[m]
                    columns_now = dot(select, getattr(r, spec.left)[m]).astype(BF16)
                    for t in range(TAPS):
                        r.h_cols[t, m * HR : (m + 1) * HR, :] = columns_now[
                            t * HR : (t + 1) * HR
                        ]

                @pl.loop(0, TAPS)
                def _(t):
                    value = dot_tn(r.h_cols[t], grad).astype(BF16)
                    for block in range(wide):
                        product[block // 2, block % 2, t] = value[
                            block * rows : (block + 1) * rows
                        ]

        def start_first(index):
            name = plan.products[index].name
            group.remote(
                getattr(r, "p_" + name).at[:, 1 - parity], getattr(r, "one_" + name), r.one_recv.at[index],
                (partner, n),
            )

        def start_second(index):
            name = plan.products[index].name
            product, one, two = getattr(r, "p_" + name), getattr(r, "one_" + name), getattr(r, "two_" + name)
            wait_bytes(one, r.one_recv.at[index])
            for q in range(pairs):
                value = product[q, parity].astype(F32) + one[q].astype(F32)
                value = value.astype(BF16)
                product[q, parity] = value
                group.remote(
                    product.at[q, parity], two.at[place], r.two_recv.at[index],
                    (2 * q + parity, n), place != q,
                )
            two[place] = product[place, parity]

        def finish(index):
            spec = plan.products[index]
            name = spec.name
            two, last = getattr(r, "two_" + name), getattr(r, "last_" + name)
            if pairs > 1:
                wait_bytes(two.at[0 : pairs - 1], r.two_recv.at[index])
            value = two[0].astype(F32)
            for q in range(1, pairs):
                value = value + two[q].astype(F32)
            width = spec.width // 2
            result = getattr(r, "out_" + name)
            shape = result.shape
            result[...] = value[..., :width].reshape(shape)
            last[...] = value[..., width:].reshape(shape)
            group.remote(last, result, r.w_recv.at[index], (w, n + 1))

        count = len(plan.products)
        for index in range(count + 2):
            if index < count:
                spec = plan.products[index]
                name = spec.name
                if spec.left_sem is not None:
                    wait_bytes(getattr(r, spec.left), r.h_recv.at[spec.left_sem])
                wait_bytes(getattr(r, "h_g_" + name), r.h_recv.at[spec.grad_sem])
                multiply(spec)
                start_first(index)
            if 0 <= index - 1 < count:
                start_second(index - 1)
            if 0 <= index - 2 < count:
                finish(index - 2)

        wait_bytes(r.o_final, r.o_recv.at[0])
        wait_bytes(r.o_input, r.o_recv.at[1])
        wait_bytes(r.o_norms, r.o_recv.at[2])
        wait_bytes(r.o_rms, r.o_recv.at[3])
        group.finish()

    @pl.when(core == 1)
    def _():
        pl.run_scoped(chain, *plan.chain_local)

    @pl.when(core == 0)
    def _():
        pl.run_scoped(helper, *plan.helper_local)

    for m in range(micros):
        r.out_block[m, 0] = r.o_final[m, 0 : HALF * HALF, :]
        r.out_input[m, 0] = r.o_input[m, 0 : FULL * FULL, :]
    norms = r.o_norms[0]
    sums = r.o_rms[0]
    for c in range(1, columns):
        norms = norms + r.o_norms[c]
        sums = sums + r.o_rms[c]
    share_width = allch // (wide * narrow)
    for target in range(narrow):

        @pl.when(n == target)
        def _(target=target):
            piece = norms[:, target * share_width : (target + 1) * share_width]
            r.out_gains[...] = piece[0]
            r.out_biases[...] = piece[1]

    square = jnp.sum(sums[0:4], axis=1, keepdims=True)
    rms = jnp.sqrt(square / (sums[4:5, 0:1] * out))
    for index in range(4):
        r.out_rms[index] = rms[index, 0]


def hand_out(results):
    count = len(results)

    def copies(*refs):
        for i in range(count - 1):
            refs[count + i][...] = refs[i][...]
        for index in range(4):
            refs[2 * count - 1][index] = refs[count - 1][index]

    in_vmem = pl.BlockSpec(memory_space=pltpu.VMEM)
    in_smem = pl.BlockSpec(memory_space=pltpu.SMEM)
    places = (in_vmem,) * (count - 1) + (in_smem,)
    return pl.pallas_call(
        copies,
        out_shape=tuple(jax.ShapeDtypeStruct(v.shape, v.dtype) for v in results),
        in_specs=places,
        out_specs=places,
        name="hand_out",
    )(*results)


def shards(
    inputs, image_sides, tile_cuts, cotangent, w_reduce1, w_spatial1, w_expand1, w_project1,
    w_reduce2, w_spatial2, w_expand2, norm_gains, norm_biases,
):
    wide = lax.axis_size(WIDE)
    narrow = lax.axis_size(NARROW)
    columns = narrow // 2
    micros = inputs.shape[0]
    slots = -(-micros // columns)
    inw, mid = w_reduce1.shape
    out = w_expand1.shape[1]
    allch = norm_gains.shape[0]
    pairs = wide // 2
    starts = (0, mid, 2 * mid, 2 * mid + out, 2 * mid + 2 * out, 3 * mid + 2 * out,
              4 * mid + 2 * out)
    widths = (mid, mid, out, out, mid, mid, out)

    def product(name, taps, depth, width, left, left_sem, grad_sem, rows):
        return SimpleNamespace(
            name=name, taps=taps, depth=depth, width=width // columns, rows=depth // wide,
            left=left, left_sem=left_sem, grad_sem=grad_sem, cells=rows,
        )

    products = (
        product("e2", 1, mid, out, "h_mix2", 4, 5, HR),
        product("s2", TAPS, mid, mid, "h_act2", 3, 6, HR),
        product("r2", 1, out, mid, "h_low1", 2, 7, HR),
        product("e1", 1, mid, out, "h_mix1", 1, 8, HR),
        product("p1", 1, inw, out, "picked", None, 9, HR),
        product("s1", TAPS, mid, mid, "h_act1", 0, 10, HR),
        product("r1", 1, inw, mid, "image", None, 11, FR),
    )
    vmem = pltpu.VMEM
    hbm = pl.BlockSpec(memory_space=pl.ANY)
    in_vmem = pl.BlockSpec(memory_space=pltpu.VMEM)
    in_smem = pl.BlockSpec(memory_space=pltpu.SMEM)

    args = dict(
        inputs=(inputs, hbm),
        image_sides=(image_sides.T, in_smem),
        tile_cuts=(tile_cuts.transpose(1, 2, 0), in_smem),
        cotangent=(cotangent, hbm),
        w_reduce1=(w_reduce1, hbm),
        w_spatial1=(w_spatial1.reshape(TAPS * mid, mid), hbm),
        w_expand1=(w_expand1, hbm),
        w_project1=(w_project1, hbm),
        w_reduce2=(w_reduce2, hbm),
        w_spatial2=(w_spatial2.reshape(TAPS * mid, mid), hbm),
        w_expand2=(w_expand2, hbm),
        gains=(norm_gains.reshape(1, allch), in_vmem),
        biases=(norm_biases.reshape(1, allch), in_vmem),
    )
    share = allch // (wide * narrow)
    outputs = dict(
        out_block=((micros, 1, HALF * HALF, out // narrow), BF16),
        out_input=((micros, 1, FULL * FULL, inw // narrow), BF16),
    )
    for spec in (products[6], products[5], products[3], products[4], products[2], products[1],
                 products[0]):
        shape = (spec.rows, spec.width // 2)
        if spec.taps > 1:
            shape = (spec.taps,) + shape
        outputs["out_" + spec.name] = (shape, F32)
    outputs["out_gains"] = ((share,), F32)
    outputs["out_biases"] = ((share,), F32)
    outputs["out_rms"] = ((4,), F32)

    scratch = dict(
        pick_back=vmem((FR, TAPS * HR), BF16),
        k_reduce1=vmem(w_reduce1.shape, BF16),
        k_spatial1=vmem((TAPS * mid, mid), BF16),
        k_expand1=vmem(w_expand1.shape, BF16),
        k_project1=vmem(w_project1.shape, BF16),
        k_reduce2=vmem(w_reduce2.shape, BF16),
        k_spatial2=vmem((TAPS * mid, mid), BF16),
        k_expand2=vmem(w_expand2.shape, BF16),
        cot_raw=vmem((slots, HALF * HALF, out), BF16),
        half=vmem((slots, HR, 128), F32),
        full=vmem((slots, FR, 128), F32),
        counts=vmem((slots, 128), F32),
        norms=vmem((2 * slots, allch), F32),
        norm_sums=vmem((2, allch), F32),
        squares=vmem((4, mid), F32),
        rms_part=vmem((8, mid), F32),
        z0=vmem((slots, FR, mid), F32),
        slope0=vmem((slots, FR, mid), F32),
        act1=vmem((slots, FR, mid), BF16),
        cols=vmem((slots * HR, TAPS * mid), BF16),
        z1=vmem((slots, HR, mid), F32),
        slope1=vmem((slots, HR, mid), F32),
        mix1=vmem((slots, HR, mid), BF16),
        z_branch=vmem((slots, HR, out), F32),
        z_short=vmem((slots, HR, out), F32),
        slope2=vmem((slots, HR, out), F32),
        low1=vmem((slots, HR, out), BF16),
        z3=vmem((slots, HR, mid), F32),
        slope3=vmem((slots, HR, mid), F32),
        act2=vmem((slots, HR, mid), BF16),
        z4=vmem((slots, HR, mid), F32),
        slope4=vmem((slots, HR, mid), F32),
        mix2=vmem((slots, HR, mid), BF16),
        z5=vmem((slots, HR, out), F32),
        u_out=vmem((slots, HR, out), F32),
        u_mid=vmem((slots, HR, mid), F32),
        final=vmem((slots, HR, out), BF16),
        g_e2=vmem((slots, HR, out), BF16),
        g_s2=vmem((slots, HR, mid), BF16),
        g_r2=vmem((slots, HR, mid), BF16),
        g_e1=vmem((slots, HR, out), BF16),
        g_p1=vmem((slots, HR, out), BF16),
        g_s1=vmem((slots, HR, mid), BF16),
        g_r1=vmem((slots, FR, mid), BF16),
        h_act1=vmem((micros, FR, mid), BF16),
        h_mix1=vmem((micros, HR, mid), BF16),
        h_low1=vmem((micros, HR, out), BF16),
        h_act2=vmem((micros, HR, mid), BF16),
        h_mix2=vmem((micros, HR, mid), BF16),
        h_cols=vmem((TAPS, micros * HR, mid), BF16),
        o_final=vmem((micros, HR, out // narrow), BF16),
        o_input=vmem((micros, FR, inw // narrow), BF16),
        o_norms=vmem((columns, 2, allch // wide), F32),
        o_rms=vmem((columns, 8, mid), F32),
    )
    stat_rows = (3, 2, 2, 2, 2, 2, 2, 2, 2, 3, 2, 2)
    stat_widths = (mid, mid, 2 * out, mid, mid, out, out, mid, mid, out, mid, mid)
    for step in range(12):
        rows = stat_rows[step] * slots + (4 if step == 7 else 0)
        scratch["stat%d" % step] = vmem((wide, rows, stat_widths[step]), F32)
    for spec in products:
        name, taps, rows, width = spec.name, spec.taps, spec.rows, spec.width
        scratch["h_g_" + name] = vmem((micros, spec.cells, width), BF16)
        scratch["p_" + name] = vmem((pairs, 2, taps, rows, width), BF16)
        scratch["one_" + name] = vmem((pairs, taps, rows, width), BF16)
        scratch["two_" + name] = vmem((pairs, taps, rows, width), BF16)
        last = (rows, width // 2) if taps == 1 else (taps, rows, width // 2)
        scratch["last_" + name] = vmem(last, F32)
    semaphores = dict(
        fetch=(16,),
        stat_send=(12,),
        stat_recv=(12,),
        chain_sends=(12 * columns * columns + 2 * slots * narrow + 2 * narrow,),
        helper_sends=(len(products) * (2 + pairs),),
        h_recv=(12,),
        o_recv=(4,),
        w_recv=(len(products),),
        one_recv=(len(products),),
        two_recv=(len(products),),
    )
    for name, shape in semaphores.items():
        scratch[name] = pltpu.SemaphoreType.DMA(shape)
    helper_local = {name: scratch.pop(name) for name in tuple(scratch) if name in ("h_cols",)
                    or name[:2] == "p_" or name[:5] == "last_"}

    def image_buffers(count):
        return dict(
            raw=vmem((count, FULL * FULL, inw), BF16),
            image=vmem((count, FR, inw), BF16),
            picked=vmem((count * HR, inw), BF16),
            pick=vmem((TAPS * HR, FR), BF16),
            tiles=vmem((count, TAPS * HR, HR), BF16),
        )

    chain_local = {name: scratch.pop(name) for name in tuple(scratch)
                   if name not in semaphores and name[:2] not in ("h_", "o_") and name[:4] not in ("one_", "two_", "stat")}
    helper_local.update(image_buffers(micros))
    chain_local.update(image_buffers(slots))
    plan = SimpleNamespace(
        chain_names=tuple(chain_local), chain_local=tuple(chain_local.values()),
        helper_names=tuple(helper_local), helper_local=tuple(helper_local.values()),
        names=tuple(args) + tuple(outputs) + tuple(scratch),
        wide=wide, narrow=narrow, micros=micros, slots=slots,
        mid=mid, out=out, inw=inw, allch=allch,
        starts=starts, layers=tuple(zip(starts, widths)), products=products,
    )
    results = pl.pallas_call(
        functools.partial(kernel, plan),
        out_shape=tuple(jax.ShapeDtypeStruct(s, d) for s, d in outputs.values()),
        in_specs=[spec for _, spec in args.values()],
        out_specs=(in_vmem,) * (len(outputs) - 1) + (in_smem,),
        scratch_shapes=list(scratch.values()),
        compiler_params=pltpu.CompilerParams(
            collective_id=0, has_side_effects=True, vmem_limit_bytes=63 * 2**20 + 2**19
        ),
        name="bottleneck_pair",
    )(*[value for value, _ in args.values()])
    return hand_out(results)


def solution(mesh):
    return jax.shard_map(
        shards,
        mesh=mesh,
        in_specs=(
            P(None, WIDE, None, None),
            P(None, WIDE),
            P(None, WIDE, None),
            P(None, WIDE, None, None),
            P(), P(), P(), P(), P(), P(), P(), P(), P(),
        ),
        out_specs=(
            P(None, WIDE, None, NARROW),
            P(None, WIDE, None, NARROW),
            P(WIDE, NARROW),
            P(None, WIDE, NARROW),
            P(WIDE, NARROW),
            P(WIDE, NARROW),
            P(WIDE, NARROW),
            P(None, WIDE, NARROW),
            P(WIDE, NARROW),
            P((WIDE, NARROW)),
            P((WIDE, NARROW)),
            P(),
        ),
        check_vma=False,
    )
```

time: 2710 us -> 140 us (0.05); the launches traced: 2680 us -> 138 us
  waiting for transfers between devices: 909 us -> 0 us
  blocking collectives: 715 us -> 0 us
  local copies, waits for them, and re-layouts: 537 us -> 0 us
  other arithmetic: 227 us -> 0 us
  starting transfers between devices: 173 us -> 0 us
  Pallas kernels: 0 us -> 137 us
  loops' own time: 70.8 us -> 0 us
    unnamed x4 -> x0, waiting for transfers between devices: 772 us -> none
    psum x25 -> x0, blocking collectives: 715 us -> none  [the longest x12 340 us: stat_sum(): return lax.psum(parts, 'wide')]
    ppermute x11 -> x0, starting transfers between devices: 167 us -> none  [from_behind(): return lax.ppermute(shard, axis, pairs)]
    pallas_call x0 -> x2, Pallas kernels: none -> 137 us  [the longest x1 135 us: shards(): pl.pallas_call(functools.partial(kernel, plan), out_shape=tuple((jax.Shap...]
    ppermute x11 -> x0, waiting for transfers between devices: 137 us -> none  [from_behind(): return lax.ppermute(shard, axis, pairs)]
    dynamic_update_slice x6 -> x0, local copies, waits for them, and re-layouts: 107 us -> none  [store_slot(): lax.dynamic_update_index_in_dim(store, jnp.where(inside, value, store[pla...]
    dynamic_slice x25 -> x0, local copies, waits for them, and re-layouts: 106 us -> none  [the longest x21 70.5 us: store_slot(): store[place_at]]
    another operation x37 -> x0, loops' own time: 70.8 us -> none  [the longest x6 42.6 us: shards(): lax.switch(chosen, back_three, env, carry, totals, weight_grads)]
  transfers between devices with their start and end apart: 15 -> 0, of which waited for: 5 -> 0; matrix products, arithmetic and copies ran while one was open for 14% -> 0% of each run, Pallas kernels for 0% -> 0%
where the time goes in v1:
time: 140 us; the launch traced here: 138 us
  Pallas kernels  137 us (98%)
    pallas_call x1, Pallas kernels, shards(): pl.pallas_call(functools.partial(kernel, plan), out_shape=tuple((jax.Shap...  135 us

profile of v1, /device:TPU:11, one launch (start us, length us, event | category | flops | bytes accessed | tf_op | source)
XLA Modules:
  0.0 138.2 jit_solution(5105785693787505362)
XLA Ops:
  0.6 134.7 %bottleneck_pair.1 = (bf16[3,1,49,512]{3,2,1,0:T(8,128)(2,1)}, bf16[3,1,196,256]{3,2,1,0:T(8,128)(2,1)}, f32[128,128]{1,0:T(8,128)}, f32[9,64,128]{2,1,0:T(8,128...) custom-call(bf16[3,1,196,1024]{3,2,1,0:T(8,128)(2,1)} %refs_0_.1, ...), custom_call_target="tpu_custom_call" | custom-call | tf_op jit(solution)/shard_map/bottleneck_pair/pallas_call | solution.py:1016
  135.4 2.7 %hand_out.1 = (bf16[3,1,49,512]{3,2,1,0:T(8,128)(2,1)}, bf16[3,1,196,256]{3,2,1,0:T(8,128)(2,1)}, f32[128,128]{1,0:T(8,128)}, f32[9,64,128]{2,1,0:T(8,128)}, f32...) custom-call(bf16[3,1,49,512]{3,2,1,0:T(8,128)(2,1)} %get-tuple-eleme, ...), custom_call_target="tpu_custom_call" | custom-call | tf_op jit(solution)/shard_map/hand_out/pallas_call | solution.py:833

commit v2 on v1

--- a/solution.py
+++ b/solution.py
@@ -21,6 +21,9 @@
 HR = 64
 FR = 208
 TAPS = 9
+STEPS = 15
+LOW_STEPS = (6, 7, 8, 9, 10, 11, 13)
+HALVING = ("e2", "r2", "e1", "p1")
 
 
 def dot(a, b):
@@ -131,18 +134,22 @@
 
 def kernel(plan, *refs):
     r = SimpleNamespace(**dict(zip(plan.names, refs)))
-    r.stat = [getattr(r, "stat%d" % step) for step in range(12)]
+    r.stat = [getattr(r, "stat%d" % step) for step in range(STEPS)]
     wide, narrow, micros, slots = plan.wide, plan.narrow, plan.micros, plan.slots
     mid, out, inw, allch = plan.mid, plan.out, plan.inw, plan.allch
-    pairs = wide // 2
+    places = wide // 2
     columns = narrow // 2
-    starts, layers = plan.starts, plan.layers
+    layers = plan.layers
     w = lax.axis_index(WIDE)
     n = lax.axis_index(NARROW)
     x = n // 2
     core = n % 2
     first_micro = x * slots
     fetch = r.fetch
+    parity = w % 2
+    place = w // 2
+    partner = w + 1 - 2 * parity
+    own_act = 0 if plan.gather else parity
 
     def micro_of(s):
         return lax.rem(first_micro + s, micros)
@@ -160,8 +167,12 @@
             barrier, inc=1, device_id=(w, lax.rem(n + d, narrow)), device_id_type=MESH
         )
 
+        pl.semaphore_signal(
+            barrier, inc=1, device_id=(partner, lax.rem(n + d, narrow)), device_id_type=MESH
+        )
+
     def pass_barrier():
-        pl.semaphore_wait(barrier, wide - 1 + narrow - 1)
+        pl.semaphore_wait(barrier, wide - 1 + 2 * (narrow - 1))
 
     def build_picks():
         rows = lax.broadcasted_iota(jnp.int32, (TAPS * HR, FR), 0)
@@ -193,12 +204,12 @@
     def fetch_image(slot, micro):
         return pltpu.make_async_copy(r.inputs.at[micro, 0], r.raw.at[slot], fetch.at[slot])
 
-    def mask_image(slot, micro):
+    def mask_image(target, slot, micro):
         mask = full_mask(micro)
         raw = jnp.concatenate(
             [r.raw[slot].astype(F32), jnp.zeros((FR - FULL * FULL, inw), F32)], axis=0
         )
-        r.image[slot] = (raw * spread(mask, inw)).astype(BF16)
+        target[...] = (raw * spread(mask, inw)).astype(BF16)
 
     def chain(*local):
         r.__dict__.update(zip(plan.chain_names, local))
@@ -262,6 +273,34 @@
         def put_pair(step, s, values, begin=0):
             put(step, 2 * s, column_sum(values), begin)
             put(step, 2 * s + 1, column_sum(values * values), begin)
+
+        def put_low(row, rows, value):
+            folds = 16 // rows
+            part = value.shape[1] // folds
+            for k in range(folds):
+                at = row * folds + k
+                r.stage[at : at + 1, 0:part] = value[:, k * part : (k + 1) * part]
+
+        def send_low(step):
+            width = r.stat[step].shape[2]
+            r.stat[step][w] = r.stage[:, 0:width].astype(BF16)
+            send_stats(step)
+
+        def wait_low(step):
+            wait_stats(step)
+            width = r.stat[step].shape[2]
+            part = r.stat[step][0].astype(F32)
+            for j in range(1, wide):
+                part = part + r.stat[step][j].astype(F32)
+            r.sums[:, 0:width] = part
+
+        def low_total(step, row, rows):
+            folds = 16 // rows
+            width = r.stat[step].shape[2]
+            first = row * folds
+            return jnp.concatenate(
+                [r.sums[first + k : first + k + 1, 0:width] for k in range(folds)], axis=1
+            )
 
         def inverse_count(s, layer):
             count = r.counts[s : s + 1, 0:1]
@@ -293,10 +332,10 @@
             _, _, scale, shift = kept(s, layer)
             return z * scale + shift
 
-        def settle_back(s, layer, step, sum_row, gain_row, begin=0):
+        def settle_back(s, layer, step, sum_u=None, sum_g=None):
             start, width = layers[layer]
-            sum_u = total(step, sum_row, begin, width)
-            sum_g = total(step, gain_row, begin, width)
+            sum_u = low_total(step, 2 * s, 2 * slots) if sum_u is None else sum_u
+            sum_g = low_total(step, 2 * s + 1, 2 * slots) if sum_g is None else sum_g
             live = jnp.where(first_micro + s < micros, 1.0, 0.0)
             for row, value in ((0, sum_g), (1, sum_u)):
                 if s == 0:
@@ -324,18 +363,26 @@
             else:
                 r.squares[index : index + 1, :] += row
 
-        def share(src, dst, recv_sem, cut=None):
+        def share(src, dst, recv_sem):
             for c in range(columns):
                 amount = min(slots, micros - c * slots)
-                if amount <= 0:
-                    continue
-                for h in range(columns):
-                    part = src.at[0:amount]
-                    if cut is not None:
-                        part = src.at[0:amount, :, h * cut : (h + 1) * cut]
+                for h in range(columns if amount > 0 else 0):
                     group.remote(
-                        part, dst.at[c * slots : c * slots + amount], recv_sem,
+                        src.at[0:amount], dst.at[c * slots : c * slots + amount], recv_sem,
                         (w, 2 * h), x == c,
+                    )
+
+        def share_grad(src, index):
+            spec = plan.products[index]
+            dst = getattr(r, "h_g_" + spec.name)
+            for c in range(columns):
+                amount = min(slots, micros - c * slots)
+                for quarter in range(narrow if amount > 0 else 0):
+                    h, v = quarter // 2, quarter % 2
+                    group.remote(
+                        src.at[0:amount, :, quarter * spec.width : (quarter + 1) * spec.width],
+                        dst.at[parity, c * slots : c * slots + amount], r.g_recv.at[index],
+                        (w - parity + v, 2 * h), x == c,
                     )
 
         def rows2(ref):
@@ -360,7 +407,7 @@
 
         for s in range(slots):
             fetch_image(s, micro_of(s)).wait()
-            mask_image(s, micro_of(s))
+            mask_image(r.image.at[s], s, micro_of(s))
         fetch_weight(0).wait()
         for s in range(slots):
             z = dot(r.image[s], r.k_reduce1[...])
@@ -380,7 +427,8 @@
         fetch_weight(2).wait()
         set_rows(r.z_short, dot(r.picked[...], r.k_project1[...]))
         for s in range(slots):
-            put_pair(2, s, r.z_short[s], out)
+            put_pair(12, s, r.z_short[s])
+        send_stats(12)
         fetch_weight(1).wait()
         wait_stats(0)
         for s in range(slots):
@@ -397,7 +445,7 @@
             r.z1[s] = rows_of(z, s)
             put_pair(1, s, rows_of(z, s) * half_wide(s, mid))
         send_stats(1)
-        share(r.act1, r.h_act1, r.h_recv.at[0])
+        share(r.act1, r.h_act1.at[own_act], r.h_recv.at[0])
         for s in range(slots):
             r.slope0[s] = gelu_slope(activation(s, 0, r.z0[s])) * spread(r.full[s], mid)
         fetch_weight(3).wait()
@@ -412,15 +460,16 @@
             r.z_branch[s] = rows_of(z, s)
             put_pair(2, s, rows_of(z, s))
         send_stats(2)
-        share(r.mix1, r.h_mix1, r.h_recv.at[1])
+        share(r.mix1, r.h_mix1.at[parity], r.h_recv.at[1])
         for s in range(slots):
             r.slope1[s] = gelu_slope(activation(s, 1, r.z1[s])) * half_wide(s, mid)
         fetch_weight(4).wait()
+        wait_stats(12)
         wait_stats(2)
 
         for s in range(slots):
-            scale, shift = settle(s, 2, 2, 0)
-            scale_short, shift_short = settle(s, 3, 2, out)
+            scale, shift = settle(s, 2, 2)
+            scale_short, shift_short = settle(s, 3, 12)
             joined = (r.z_branch[s] * scale + shift) + (
                 r.z_short[s] * scale_short + shift_short
             )
@@ -432,7 +481,7 @@
             r.z3[s] = rows_of(z, s)
             put_pair(3, s, rows_of(z, s))
         send_stats(3)
-        share(r.low1, r.h_low1, r.h_recv.at[2])
+        share(r.low1, r.h_low1.at[parity], r.h_recv.at[2])
         for s in range(slots):
             mask = half_wide(s, out)
             branch = activation(s, 2, r.z_branch[s])
@@ -455,7 +504,7 @@
             r.z4[s] = rows_of(z, s)
             put_pair(4, s, rows_of(z, s) * half_wide(s, mid))
         send_stats(4)
-        share(r.act2, r.h_act2, r.h_recv.at[3])
+        share(r.act2, r.h_act2.at[own_act], r.h_recv.at[3])
         for s in range(slots):
             r.slope3[s] = gelu_slope(activation(s, 4, r.z3[s])) * half_wide(s, mid)
         fetch_weight(6).wait()
@@ -470,7 +519,7 @@
             r.z5[s] = rows_of(z, s)
             put_pair(5, s, rows_of(z, s))
         send_stats(5)
-        share(r.mix2, r.h_mix2, r.h_recv.at[4])
+        share(r.mix2, r.h_mix2.at[parity], r.h_recv.at[4])
         for s in range(slots):
             r.slope4[s] = gelu_slope(activation(s, 5, r.z4[s])) * half_wide(s, mid)
             fetch_cotangent(s).wait()
@@ -484,9 +533,9 @@
             )
             u = gelu_slope(joined) * cot * half_wide(s, out)
             r.u_out[s] = u
-            put(6, 2 * s, column_sum(u))
-            put(6, 2 * s + 1, column_sum(u * normed(s, 6, r.z5[s])))
-        send_stats(6)
+            put_low(2 * s, 2 * slots, column_sum(u))
+            put_low(2 * s + 1, 2 * slots, column_sum(u * normed(s, 6, r.z5[s])))
+        send_low(6)
         for s in range(slots):
             mask = half_wide(s, out)
             branch = activation(s, 6, r.z5[s])
@@ -503,32 +552,33 @@
                     src, dst, r.o_recv.at[0], (w, target),
                     (first_micro + s < micros) & (n != target),
                 )
-        for index in range(4):
-            put(7, 2 * slots + index, r.squares[index : index + 1, :])
-        wait_stats(6)
-
-        for s in range(slots):
-            k0, k1, k2 = settle_back(s, 6, 6, 2 * s, 2 * s + 1)
+        r.stat[14][w] = r.squares[...]
+        send_stats(14)
+        wait_low(6)
+
+        for s in range(slots):
+            k0, k1, k2 = settle_back(s, 6, 6)
             grad = (k0 * r.u_out[s] + k1 + k2 * r.z5[s]) * half_wide(s, out)
             r.g_e2[s] = grad.astype(BF16)
         back = dot_nt(rows2(r.g_e2), r.k_expand2[...]).astype(BF16).astype(F32)
         for s in range(slots):
             u = rows_of(back, s) * r.slope4[s]
             r.u_mid[s] = u
-            put(7, 2 * s, column_sum(u))
-            put(7, 2 * s + 1, column_sum(u * normed(s, 5, r.z4[s])))
-        send_stats(7)
-        share(r.g_e2, r.h_g_e2, r.h_recv.at[5], out // columns)
-        wait_stats(7)
+            put_low(2 * s, 2 * slots, column_sum(u))
+            put_low(2 * s + 1, 2 * slots, column_sum(u * normed(s, 5, r.z4[s])))
+        send_low(7)
+        share_grad(r.g_e2, 0)
+        wait_low(7)
+        wait_stats(14)
         for index in range(4):
-            r.rms_part[index : index + 1, :] = total(7, 2 * slots + index)
+            r.rms_part[index : index + 1, :] = total(14, index)
         count = r.counts[0:1, :]
         for s in range(1, slots):
             count = count + live_row(s, r.counts[s : s + 1, :])
         r.rms_part[4:5, :] = spread(count, mid)
 
         for s in range(slots):
-            k0, k1, k2 = settle_back(s, 5, 7, 2 * s, 2 * s + 1)
+            k0, k1, k2 = settle_back(s, 5, 7)
             grad = (k0 * r.u_mid[s] + k1 + k2 * r.z4[s]) * half_wide(s, mid)
             r.g_s2[s] = grad.astype(BF16)
             gather_tiles(s, r.g_s2[s], r.tiles[s])
@@ -543,52 +593,56 @@
         for s in range(slots):
             u = rows_of(back, s) * r.slope3[s]
             r.u_mid[s] = u
-            put(8, 2 * s, column_sum(u))
-            put(8, 2 * s + 1, column_sum(u * normed(s, 4, r.z3[s])))
-        send_stats(8)
-        share(r.g_s2, r.h_g_s2, r.h_recv.at[6], mid // columns)
-        wait_stats(8)
-
-        for s in range(slots):
-            k0, k1, k2 = settle_back(s, 4, 8, 2 * s, 2 * s + 1)
+            put_low(2 * s, 2 * slots, column_sum(u))
+            put_low(2 * s + 1, 2 * slots, column_sum(u * normed(s, 4, r.z3[s])))
+        send_low(8)
+        share_grad(r.g_s2, 1)
+        wait_low(8)
+
+        for s in range(slots):
+            k0, k1, k2 = settle_back(s, 4, 8)
             grad = (k0 * r.u_mid[s] + k1 + k2 * r.z3[s]) * half_wide(s, mid)
             r.g_r2[s] = grad.astype(BF16)
         back = dot_nt(rows2(r.g_r2), r.k_reduce2[...])
         for s in range(slots):
             u = (rows_of(back, s) + r.u_out[s].astype(BF16).astype(F32)) * r.slope2[s]
             r.u_out[s] = u
-            put(9, 3 * s, column_sum(u))
-            put(9, 3 * s + 1, column_sum(u * normed(s, 2, r.z_branch[s])))
-            put(9, 3 * s + 2, column_sum(u * normed(s, 3, r.z_short[s])))
-        send_stats(9)
-        share(r.g_r2, r.h_g_r2, r.h_recv.at[7], mid // columns)
-        wait_stats(9)
-
-        for s in range(slots):
-            k0, k1, k2 = settle_back(s, 2, 9, 3 * s, 3 * s + 1)
+            put_low(2 * s, 2 * slots, column_sum(u))
+            put_low(2 * s + 1, 2 * slots, column_sum(u * normed(s, 2, r.z_branch[s])))
+        send_low(9)
+        for s in range(slots):
+            put_low(s, slots, column_sum(r.u_out[s] * normed(s, 3, r.z_short[s])))
+        send_low(13)
+        share_grad(r.g_r2, 2)
+        wait_low(9)
+
+        for s in range(slots):
+            k0, k1, k2 = settle_back(s, 2, 9)
             grad = (k0 * r.u_out[s] + k1 + k2 * r.z_branch[s]) * half_wide(s, out)
             r.g_e1[s] = grad.astype(BF16)
         back = dot_nt(rows2(r.g_e1), r.k_expand1[...]).astype(BF16).astype(F32)
         for s in range(slots):
             u = rows_of(back, s) * r.slope1[s]
             r.u_mid[s] = u
-            put(10, 2 * s, column_sum(u))
-            put(10, 2 * s + 1, column_sum(u * normed(s, 1, r.z1[s])))
-        send_stats(10)
-        share(r.g_e1, r.h_g_e1, r.h_recv.at[8], out // columns)
-        for s in range(slots):
-            k0, k1, k2 = settle_back(s, 3, 9, 3 * s, 3 * s + 2)
+            put_low(2 * s, 2 * slots, column_sum(u))
+            put_low(2 * s + 1, 2 * slots, column_sum(u * normed(s, 1, r.z1[s])))
+        send_low(10)
+        sums_u = [low_total(9, 2 * s, 2 * slots) for s in range(slots)]
+        wait_low(13)
+        for s in range(slots):
+            k0, k1, k2 = settle_back(s, 3, 13, sums_u[s], low_total(13, s, slots))
             grad = (k0 * r.u_out[s] + k1 + k2 * r.z_short[s]) * half_wide(s, out)
             r.g_p1[s] = grad.astype(BF16)
-        share(r.g_p1, r.h_g_p1, r.h_recv.at[9], out // columns)
+        share_grad(r.g_p1, 4)
+        share_grad(r.g_e1, 3)
         build_pick_back()
         r.picked[...] = dot_nt(rows2(r.g_p1), r.k_project1[...]).astype(
             BF16
         )
-        wait_stats(10)
-
-        for s in range(slots):
-            k0, k1, k2 = settle_back(s, 1, 10, 2 * s, 2 * s + 1)
+        wait_low(10)
+
+        for s in range(slots):
+            k0, k1, k2 = settle_back(s, 1, 10)
             grad = (k0 * r.u_mid[s] + k1 + k2 * r.z1[s]) * half_wide(s, mid)
             r.g_s1[s] = grad.astype(BF16)
         g_rows = rows2(r.g_s1)
@@ -603,17 +657,17 @@
             )
             u = dot(r.pick_back[...], back) * r.slope0[s]
             r.slope0[s] = u
-            put(11, 2 * s, column_sum(u))
-            put(11, 2 * s + 1, column_sum(u * normed(s, 0, r.z0[s])))
-        send_stats(11)
-        share(r.g_s1, r.h_g_s1, r.h_recv.at[10], mid // columns)
-        wait_stats(11)
-
-        for s in range(slots):
-            k0, k1, k2 = settle_back(s, 0, 11, 2 * s, 2 * s + 1)
+            put_low(2 * s, 2 * slots, column_sum(u))
+            put_low(2 * s + 1, 2 * slots, column_sum(u * normed(s, 0, r.z0[s])))
+        send_low(11)
+        share_grad(r.g_s1, 5)
+        wait_low(11)
+
+        for s in range(slots):
+            k0, k1, k2 = settle_back(s, 0, 11)
             grad = (k0 * r.slope0[s] + k1 + k2 * r.z0[s]) * spread(r.full[s], mid)
             r.g_r1[s] = grad.astype(BF16)
-        share(r.g_r1, r.h_g_r1, r.h_recv.at[11], mid // columns)
+        share_grad(r.g_r1, 6)
         section = allch // wide
         own = pl.ds(pl.multiple_of(w * section, 128), section)
         for target in range(narrow):
@@ -664,127 +718,292 @@
 
         wait_bytes(r.o_norms.at[0 : columns - 1], r.o_recv.at[2])
         wait_bytes(r.o_rms.at[0 : columns - 1], r.o_recv.at[3])
+        wait_products()
+        group.finish()
+        for step in range(STEPS):
+            wait_bytes(r.stat[step].at[pl.ds(0, wide - 1)], r.stat_send.at[step])
+
+    def wait_products():
         for index, spec in enumerate(plan.products):
             wait_bytes(getattr(r, "out_" + spec.name), r.w_recv.at[index])
-        group.finish()
-        for step in range(12):
-            wait_bytes(r.stat[step].at[pl.ds(0, wide - 1)], r.stat_send.at[step])
 
     def helper(*local):
         r.__dict__.update(zip(plan.helper_names, local))
         group = Group(r.helper_sends)
-        parity = w % 2
-        place = w // 2
-        partner = w + 1 - 2 * parity
+        low, high = place % 2, place // 2
+
+        def relay(ref, sem):
+            group.remote(ref.at[parity], ref.at[parity], r.y_recv.at[sem], (partner, n))
+
+        def arrived(ref, sem):
+            wait_bytes(ref.at[0], r.y_recv.at[sem])
+
+        def scatter(src, dst, sem):
+            for q in range(places):
+                part = src.at[:, :, q * 128 : (q + 1) * 128]
+                group.remote(
+                    part, dst.at[place, parity], r.z_recv.at[sem], (2 * q + parity, n), place != q
+                )
+
+                @pl.when(place == q)
+                def _(q=q):
+                    dst[q, parity] = src[:, :, q * 128 : (q + 1) * 128]
+
+        def forward(ref, sem):
+            if places > 1:
+                wait_bytes(ref.at[0 : places - 1, 0], r.z_recv.at[sem])
+            group.remote(
+                ref.at[:, parity], ref.at[:, parity], r.y_recv.at[sem], (partner, n)
+            )
+
+        def forwarded(ref, sem):
+            wait_bytes(ref.at[:, 0], r.y_recv.at[sem])
+
+        def tile_base():
+            rows = lax.broadcasted_iota(jnp.int32, (TAPS * HR, HR), 0)
+            cells = lax.broadcasted_iota(jnp.int32, (TAPS * HR, HR), 1)
+            a, b = tap_of(rows)
+            p = lax.bitwise_and(rows, 63)
+            i, j = half_cell(p)
+            ti, tj = i + a, j + b
+            inside = (p < HALF * HALF) & (ti >= 0) & (ti < HALF) & (tj >= 0) & (tj < HALF)
+            r.t_base[...] = one_zero(inside & (cells == ti * HALF + tj))
+            r.t_row[...] = jnp.where(a != 0, jnp.maximum(i, ti), -1).astype(F32)
+            r.t_col[...] = jnp.where(b != 0, jnp.maximum(j, tj), -1).astype(F32)
+
+        def tiles_at(q, v, m):
+            keep = (r.t_row[...] != r.cuts[q, v, 2 * m : 2 * m + 1, 0:HR]) & (
+                r.t_col[...] != r.cuts[q, v, 2 * m + 1 : 2 * m + 2, 0:HR]
+            )
+            return jnp.where(keep, r.t_base[...], 0.0).astype(BF16)
+
+        def strided_columns(cols, source):
+            @pl.loop(0, places)
+            def _(q):
+                for v in range(2):
+                    grids = jnp.concatenate([source[q, v, m] for m in range(micros)], axis=1)
+                    picked = dot(r.pick[...], grids).astype(BF16)
+                    for m in range(micros):
+                        row = pl.multiple_of(((q * 2 + v) * micros + m) * HR, HR)
+                        for t in range(TAPS):
+                            cols[pl.ds(row, HR), t * 128 : (t + 1) * 128] = picked[
+                                t * HR : (t + 1) * HR, m * 128 : (m + 1) * 128
+                            ]
+
+        def tile_columns(cols, source):
+            @pl.loop(0, places)
+            def _(q):
+                for v in range(2):
+                    for m in range(micros):
+                        row = pl.multiple_of(((q * 2 + v) * micros + m) * HR, HR)
+                        picked = dot(tiles_at(q, v, m), source[q, v, m]).astype(BF16)
+                        for t in range(TAPS):
+                            cols[pl.ds(row, HR), t * 128 : (t + 1) * 128] = picked[
+                                t * HR : (t + 1) * HR
+                            ]
+
+        def pair_columns(name, source):
+            for v in range(2):
+                for m in range(micros):
+                    select = r.pick[...] if name == "s1" else tiles_at(place, v, m)
+                    picked = dot(select, source[v, m]).astype(BF16)
+                    for t in range(TAPS):
+                        r.h_cols[t, v, m] = picked[t * HR : (t + 1) * HR]
+
+        def flat(value):
+            return value.reshape(math.prod(value.shape[:-1]), value.shape[-1])
+
+        def store_blocks(product, tap, begin, value, deep, halving):
+            step = min(deep, value.shape[0])
+            for b in range(0, value.shape[0], step):
+                row = begin + b
+                at = pl.ds(row % deep, step)
+                block = row // deep
+                if halving:
+                    product[block // 2, block % 2, tap, at, :] = value[b : b + step]
+                else:
+                    product[block, tap, at, :] = value[b : b + step]
+
+        def multiply(spec):
+            grad = flat(getattr(r, "h_g_" + spec.name)[...])
+            product = getattr(r, "p_" + spec.name)
+            deep = spec.depth // places
+            chunk = min(256, spec.depth)
+            if spec.taps == 1:
+                left = getattr(r, spec.left)
+                for begin in range(0, spec.depth, chunk):
+                    value = dot_tn(flat(left[..., begin : begin + chunk]), grad).astype(BF16)
+                    store_blocks(product, 0, begin, value, deep, spec.halving)
+            else:
+                pair_columns(spec.name, getattr(r, spec.left))
+
+                @pl.loop(0, TAPS)
+                def _(t):
+                    for begin in range(0, spec.depth, chunk):
+                        value = dot_tn(
+                            flat(r.h_cols[t, :, :, :, begin : begin + chunk]), grad
+                        ).astype(BF16)
+                        store_blocks(product, t, begin, value, deep, spec.halving)
+
+        def start(index):
+            spec = plan.products[index]
+            grad = getattr(r, "h_g_" + spec.name)
+            wait_bytes(grad, r.g_recv.at[index])
+            if spec.gathered:
+                source, target = grad, getattr(r, "ga_" + spec.name)
+            else:
+                multiply(spec)
+                source, target = getattr(r, "p_" + spec.name), getattr(r, "two_" + spec.name)
+            if spec.halving:
+                group.remote(
+                    source.at[:, 1 - low], getattr(r, "one_" + spec.name),
+                    r.one_recv.at[index], (2 * (place + 1 - 2 * low) + parity, n),
+                )
+                return
+            for q in range(places):
+                group.remote(
+                    source if spec.gathered else source.at[q], target.at[place],
+                    r.two_recv.at[index], (2 * q + parity, n), place != q,
+                )
+            target[place] = source[...] if spec.gathered else source[place]
+
+        def middle(index):
+            spec = plan.products[index]
+            if not spec.halving:
+                return
+            source, one = getattr(r, "p_" + spec.name), getattr(r, "one_" + spec.name)
+            wait_bytes(one, r.one_recv.at[index])
+            far = source[1 - high, low].astype(F32) + one[1 - high].astype(F32)
+            source[1 - high, low] = far.astype(BF16)
+            group.remote(
+                source.at[1 - high, low], getattr(r, "two_" + spec.name), r.two_recv.at[index],
+                (2 * (place + 2 - 4 * high) + parity, n),
+            )
+
+        def finish(index):
+            spec = plan.products[index]
+            rows = spec.rows
+            last = getattr(r, "last_" + spec.name)
+            target = getattr(r, ("ga_" if spec.gathered else "two_") + spec.name)
+            if spec.halving:
+                wait_bytes(target, r.two_recv.at[index])
+            elif places > 1:
+                wait_bytes(target.at[0 : places - 1], r.two_recv.at[index])
+            if spec.gathered:
+                cols = getattr(r, "cols_" + spec.name)
+                value = dot_tn(flat(target[...]), cols[...])
+                for t in range(TAPS):
+                    tap = value[:, t * 128 : (t + 1) * 128].T
+                    for half in range(2):
+                        last[half, t] = tap[half * rows : (half + 1) * rows]
+            else:
+                if spec.halving:
+                    value = getattr(r, "p_" + spec.name)[high, low].astype(F32)
+                    value = value + getattr(r, "one_" + spec.name)[high].astype(F32)
+                    value = value + target[...].astype(F32)
+                else:
+                    value = target[0].astype(F32)
+                    for q in range(1, places):
+                        value = value + target[q].astype(F32)
+                for half in range(2):
+                    part = value[:, half * rows : (half + 1) * rows]
+                    last[half] = part if spec.taps > 1 else part[0]
+            result = getattr(r, "out_" + spec.name)
+
+            @pl.when(parity == 0)
+            def _():
+                result[...] = last[0]
+
+            sem = r.w_recv.at[index]
+            group.remote(last.at[1], result, sem, (partner, n), parity == 0)
+            group.remote(last.at[0], result, sem, (partner, n + 1), parity == 1)
+            group.remote(last.at[1], result, sem, (w, n + 1), parity == 1)
 
         for m in range(micros):
             fetch_image(m, m).start()
         build_picks()
+        tile_base()
         for m in range(micros):
-            build_tiles(m, m)
+            for k in range(2):
+                cut = jnp.full((1, 128), r.tile_cuts[0, k, m], jnp.int32).astype(F32)
+                r.cuts[place, parity, 2 * m + k : 2 * m + k + 1, :] = cut
         for m in range(micros):
             fetch_image(m, m).wait()
-            mask_image(m, m)
-        centre = r.pick[4 * HR : 5 * HR, :]
-        for m in range(micros):
-            r.picked[m * HR : (m + 1) * HR, :] = dot(centre, r.image[m]).astype(BF16)
+            mask_image(r.h_image.at[parity, m], m, m)
         pass_barrier()
-
-        def tall(ref):
-            value = ref[...]
-            return value.reshape(value.shape[0] * value.shape[1], value.shape[2])
-
-        def multiply(spec):
-            name, rows = spec.name, spec.rows
-            grad = tall(getattr(r, "h_g_" + name))
-            product = getattr(r, "p_" + name)
-            if spec.taps == 1:
-                left = r.picked if name == "p1" else None
-                chunk = min(256, spec.depth)
-                for begin in range(0, spec.depth, chunk):
-                    if name == "p1":
-                        piece = left[:, begin : begin + chunk]
-                    else:
-                        source = getattr(r, spec.left)
-                        piece = source[:, :, begin : begin + chunk]
-                        piece = piece.reshape(piece.shape[0] * piece.shape[1], chunk)
-                    value = dot_tn(piece, grad).astype(BF16)
-                    for b in range(chunk // rows):
-                        block = begin // rows + b
-                        product[block // 2, block % 2, 0] = value[b * rows : (b + 1) * rows]
-            else:
-                for m in range(micros):
-                    select = r.pick[...] if name == "s1" else r.tiles[m]
-                    columns_now = dot(select, getattr(r, spec.left)[m]).astype(BF16)
-                    for t in range(TAPS):
-                        r.h_cols[t, m * HR : (m + 1) * HR, :] = columns_now[
-                            t * HR : (t + 1) * HR
-                        ]
-
-                @pl.loop(0, TAPS)
-                def _(t):
-                    value = dot_tn(r.h_cols[t], grad).astype(BF16)
-                    for block in range(wide):
-                        product[block // 2, block % 2, t] = value[
-                            block * rows : (block + 1) * rows
-                        ]
-
-        def start_first(index):
-            name = plan.products[index].name
-            group.remote(
-                getattr(r, "p_" + name).at[:, 1 - parity], getattr(r, "one_" + name), r.one_recv.at[index],
-                (partner, n),
-            )
-
-        def start_second(index):
-            name = plan.products[index].name
-            product, one, two = getattr(r, "p_" + name), getattr(r, "one_" + name), getattr(r, "two_" + name)
-            wait_bytes(one, r.one_recv.at[index])
-            for q in range(pairs):
-                value = product[q, parity].astype(F32) + one[q].astype(F32)
-                value = value.astype(BF16)
-                product[q, parity] = value
+        relay(r.h_image, 0)
+        if plan.gather:
+            for q in range(places):
                 group.remote(
-                    product.at[q, parity], two.at[place], r.two_recv.at[index],
+                    r.cuts.at[place, parity], r.cuts.at[place, parity], r.z_recv.at[1],
                     (2 * q + parity, n), place != q,
                 )
-            two[place] = product[place, parity]
-
-        def finish(index):
-            spec = plan.products[index]
-            name = spec.name
-            two, last = getattr(r, "two_" + name), getattr(r, "last_" + name)
-            if pairs > 1:
-                wait_bytes(two.at[0 : pairs - 1], r.two_recv.at[index])
-            value = two[0].astype(F32)
-            for q in range(1, pairs):
-                value = value + two[q].astype(F32)
-            width = spec.width // 2
-            result = getattr(r, "out_" + name)
-            shape = result.shape
-            result[...] = value[..., :width].reshape(shape)
-            last[...] = value[..., width:].reshape(shape)
-            group.remote(last, result, r.w_recv.at[index], (w, n + 1))
-
-        count = len(plan.products)
-        for index in range(count + 2):
-            if index < count:
-                spec = plan.products[index]
-                name = spec.name
-                if spec.left_sem is not None:
-                    wait_bytes(getattr(r, spec.left), r.h_recv.at[spec.left_sem])
-                wait_bytes(getattr(r, "h_g_" + name), r.h_recv.at[spec.grad_sem])
-                multiply(spec)
-                start_first(index)
-            if 0 <= index - 1 < count:
-                start_second(index - 1)
-            if 0 <= index - 2 < count:
-                finish(index - 2)
+        else:
+            relay(r.cuts.at[place], 1)
+        wait_bytes(r.h_act1.at[0], r.h_recv.at[0])
+        if plan.gather:
+            scatter(r.h_act1.at[0], r.sp_act1, 2)
+            forward(r.cuts, 1)
+        else:
+            relay(r.h_act1, 2)
+        wait_bytes(r.h_mix1.at[0], r.h_recv.at[1])
+        relay(r.h_mix1, 3)
+        if plan.gather:
+            forward(r.sp_act1, 2)
+        wait_bytes(r.h_low1.at[0], r.h_recv.at[2])
+        relay(r.h_low1, 4)
+        if plan.gather:
+            forwarded(r.sp_act1, 2)
+            strided_columns(r.cols_s1, r.sp_act1)
+        arrived(r.h_image, 0)
+        centre = r.pick[4 * HR : 5 * HR, :]
+        for v in range(2):
+            for m in range(micros):
+                r.h_picked[v, m] = dot(centre, r.h_image[v, m]).astype(BF16)
+        wait_bytes(r.h_act2.at[0], r.h_recv.at[3])
+        if plan.gather:
+            scatter(r.h_act2.at[0], r.sp_act2, 5)
+        else:
+            relay(r.h_act2, 5)
+        wait_bytes(r.h_mix2.at[0], r.h_recv.at[4])
+        relay(r.h_mix2, 6)
+        if plan.gather:
+            forward(r.sp_act2, 5)
+            forwarded(r.cuts, 1)
+            forwarded(r.sp_act2, 5)
+            tile_columns(r.cols_s2, r.sp_act2)
+        else:
+            arrived(r.cuts.at[0], 1)
+            arrived(r.h_act1, 2)
+            arrived(r.h_act2, 5)
+        arrived(r.h_mix1, 3)
+        arrived(r.h_low1, 4)
+        arrived(r.h_mix2, 6)
+
+        start(0)
+        middle(0)
+        start(1)
+        start(2)
+        middle(2)
+        start(4)
+        start(3)
+        middle(4)
+        middle(3)
+        start(5)
+        start(6)
+        finish(0)
+        finish(1)
+        finish(2)
+        finish(4)
+        finish(3)
+        finish(5)
+        finish(6)
 
         wait_bytes(r.o_final, r.o_recv.at[0])
         wait_bytes(r.o_input, r.o_recv.at[1])
         wait_bytes(r.o_norms, r.o_recv.at[2])
         wait_bytes(r.o_rms, r.o_recv.at[3])
+        pl.when(parity == 1)(wait_products)
         group.finish()
 
     @pl.when(core == 1)
@@ -851,25 +1070,27 @@
     inw, mid = w_reduce1.shape
     out = w_expand1.shape[1]
     allch = norm_gains.shape[0]
-    pairs = wide // 2
+    places = wide // 2
+    gather = mid // places == 128
     starts = (0, mid, 2 * mid, 2 * mid + out, 2 * mid + 2 * out, 3 * mid + 2 * out,
               4 * mid + 2 * out)
     widths = (mid, mid, out, out, mid, mid, out)
 
-    def product(name, taps, depth, width, left, left_sem, grad_sem, rows):
+    def product(name, taps, depth, width, left, rows):
         return SimpleNamespace(
-            name=name, taps=taps, depth=depth, width=width // columns, rows=depth // wide,
-            left=left, left_sem=left_sem, grad_sem=grad_sem, cells=rows,
+            name=name, taps=taps, depth=depth, width=width // narrow, rows=depth // wide,
+            left=left, cells=rows, gathered=gather and taps > 1,
+            halving=places == 4 and name in HALVING,
         )
 
     products = (
-        product("e2", 1, mid, out, "h_mix2", 4, 5, HR),
-        product("s2", TAPS, mid, mid, "h_act2", 3, 6, HR),
-        product("r2", 1, out, mid, "h_low1", 2, 7, HR),
-        product("e1", 1, mid, out, "h_mix1", 1, 8, HR),
-        product("p1", 1, inw, out, "picked", None, 9, HR),
-        product("s1", TAPS, mid, mid, "h_act1", 0, 10, HR),
-        product("r1", 1, inw, mid, "image", None, 11, FR),
+        product("e2", 1, mid, out, "h_mix2", HR),
+        product("s2", TAPS, mid, mid, "h_act2", HR),
+        product("r2", 1, out, mid, "h_low1", HR),
+        product("e1", 1, mid, out, "h_mix1", HR),
+        product("p1", 1, inw, out, "h_picked", HR),
+        product("s1", TAPS, mid, mid, "h_act1", HR),
+        product("r1", 1, inw, mid, "h_image", FR),
     )
     vmem = pltpu.VMEM
     hbm = pl.BlockSpec(memory_space=pl.ANY)
@@ -898,7 +1119,7 @@
     )
     for spec in (products[6], products[5], products[3], products[4], products[2], products[1],
                  products[0]):
-        shape = (spec.rows, spec.width // 2)
+        shape = (spec.rows, spec.width)
         if spec.taps > 1:
             shape = (spec.taps,) + shape
         outputs["out_" + spec.name] = (shape, F32)
@@ -922,6 +1143,8 @@
         norms=vmem((2 * slots, allch), F32),
         norm_sums=vmem((2, allch), F32),
         squares=vmem((4, mid), F32),
+        stage=vmem((16, out // 4), F32),
+        sums=vmem((16, out // 4), F32),
         rms_part=vmem((8, mid), F32),
         z0=vmem((slots, FR, mid), F32),
         slope0=vmem((slots, FR, mid), F32),
@@ -951,67 +1174,90 @@
         g_p1=vmem((slots, HR, out), BF16),
         g_s1=vmem((slots, HR, mid), BF16),
         g_r1=vmem((slots, FR, mid), BF16),
-        h_act1=vmem((micros, FR, mid), BF16),
-        h_mix1=vmem((micros, HR, mid), BF16),
-        h_low1=vmem((micros, HR, out), BF16),
-        h_act2=vmem((micros, HR, mid), BF16),
-        h_mix2=vmem((micros, HR, mid), BF16),
-        h_cols=vmem((TAPS, micros * HR, mid), BF16),
+        h_act1=vmem((1 if gather else 2, micros, FR, mid), BF16),
+        h_mix1=vmem((2, micros, HR, mid), BF16),
+        h_low1=vmem((2, micros, HR, out), BF16),
+        h_act2=vmem((1 if gather else 2, micros, HR, mid), BF16),
+        h_mix2=vmem((2, micros, HR, mid), BF16),
+        h_image=vmem((2, micros, FR, inw), BF16),
+        cuts=vmem((places, 2, 8, 128), F32),
         o_final=vmem((micros, HR, out // narrow), BF16),
         o_input=vmem((micros, FR, inw // narrow), BF16),
         o_norms=vmem((columns, 2, allch // wide), F32),
         o_rms=vmem((columns, 8, mid), F32),
     )
-    stat_rows = (3, 2, 2, 2, 2, 2, 2, 2, 2, 3, 2, 2)
-    stat_widths = (mid, mid, 2 * out, mid, mid, out, out, mid, mid, out, mid, mid)
-    for step in range(12):
-        rows = stat_rows[step] * slots + (4 if step == 7 else 0)
-        scratch["stat%d" % step] = vmem((wide, rows, stat_widths[step]), F32)
+    stat_rows = (3, 2, 2, 2, 2, 2, 2, 2, 2, 2, 2, 2, 2, 1, 2)
+    stat_widths = (mid, mid, out, mid, mid, out, out, mid, mid, out, mid, mid, out, out, mid)
+    for step in range(STEPS):
+        rows, width = stat_rows[step] * slots, stat_widths[step]
+        if step in LOW_STEPS:
+            scratch["stat%d" % step] = vmem((wide, 16, rows * width // 16), BF16)
+        else:
+            scratch["stat%d" % step] = vmem((wide, rows, width), F32)
+    helper_local = dict(
+        raw=vmem((micros, FULL * FULL, inw), BF16),
+        pick=vmem((TAPS * HR, FR), BF16),
+        h_picked=vmem((2, micros, HR, inw), BF16),
+        t_base=vmem((TAPS * HR, HR), F32),
+        t_row=vmem((TAPS * HR, HR), F32),
+        t_col=vmem((TAPS * HR, HR), F32),
+    )
+    if gather:
+        scratch["sp_act1"] = vmem((places, 2, micros, FR, 128), BF16)
+        scratch["sp_act2"] = vmem((places, 2, micros, HR, 128), BF16)
+    else:
+        helper_local["h_cols"] = vmem((TAPS, 2, micros, HR, mid), BF16)
     for spec in products:
         name, taps, rows, width = spec.name, spec.taps, spec.rows, spec.width
-        scratch["h_g_" + name] = vmem((micros, spec.cells, width), BF16)
-        scratch["p_" + name] = vmem((pairs, 2, taps, rows, width), BF16)
-        scratch["one_" + name] = vmem((pairs, taps, rows, width), BF16)
-        scratch["two_" + name] = vmem((pairs, taps, rows, width), BF16)
-        last = (rows, width // 2) if taps == 1 else (taps, rows, width // 2)
-        scratch["last_" + name] = vmem(last, F32)
+        scratch["h_g_" + name] = vmem((2, micros, spec.cells, width), BF16)
+        if spec.gathered:
+            scratch["ga_" + name] = vmem((places, 2, micros, HR, width), BF16)
+            helper_local["cols_" + name] = vmem((places * 2 * micros * HR, TAPS * 128), BF16)
+        else:
+            block = (taps, 2 * rows, width)
+            if spec.halving:
+                scratch["one_" + name] = vmem((2,) + block, BF16)
+                scratch["two_" + name] = vmem(block, BF16)
+                helper_local["p_" + name] = vmem((2, 2) + block, BF16)
+            else:
+                scratch["two_" + name] = vmem((places,) + block, BF16)
+                helper_local["p_" + name] = vmem((places,) + block, BF16)
+        last = (2, rows, width) if taps == 1 else (2, taps, rows, width)
+        helper_local["last_" + name] = vmem(last, F32)
     semaphores = dict(
         fetch=(16,),
-        stat_send=(12,),
-        stat_recv=(12,),
-        chain_sends=(12 * columns * columns + 2 * slots * narrow + 2 * narrow,),
-        helper_sends=(len(products) * (2 + pairs),),
-        h_recv=(12,),
+        stat_send=(STEPS,),
+        stat_recv=(STEPS,),
+        chain_sends=(7 * columns * narrow + 5 * columns * columns + 2 * slots * narrow + 2 * narrow,),
+        helper_sends=(7 * (places + 3) + 3 * places + 16,),
+        h_recv=(5,),
+        g_recv=(7,),
+        y_recv=(7,),
+        z_recv=(7,),
         o_recv=(4,),
-        w_recv=(len(products),),
-        one_recv=(len(products),),
-        two_recv=(len(products),),
+        w_recv=(7,),
+        one_recv=(7,),
+        two_recv=(7,),
     )
     for name, shape in semaphores.items():
         scratch[name] = pltpu.SemaphoreType.DMA(shape)
-    helper_local = {name: scratch.pop(name) for name in tuple(scratch) if name in ("h_cols",)
-                    or name[:2] == "p_" or name[:5] == "last_"}
-
-    def image_buffers(count):
-        return dict(
-            raw=vmem((count, FULL * FULL, inw), BF16),
-            image=vmem((count, FR, inw), BF16),
-            picked=vmem((count * HR, inw), BF16),
-            pick=vmem((TAPS * HR, FR), BF16),
-            tiles=vmem((count, TAPS * HR, HR), BF16),
-        )
-
+    shared = ("h_", "o_", "sp", "ga", "cu", "on", "tw")
     chain_local = {name: scratch.pop(name) for name in tuple(scratch)
-                   if name not in semaphores and name[:2] not in ("h_", "o_") and name[:4] not in ("one_", "two_", "stat")}
-    helper_local.update(image_buffers(micros))
-    chain_local.update(image_buffers(slots))
+                   if name not in semaphores and name[:2] not in shared and name[:4] != "stat"}
+    chain_local.update(
+        raw=vmem((slots, FULL * FULL, inw), BF16),
+        image=vmem((slots, FR, inw), BF16),
+        picked=vmem((slots * HR, inw), BF16),
+        pick=vmem((TAPS * HR, FR), BF16),
+        tiles=vmem((slots, TAPS * HR, HR), BF16),
+    )
     plan = SimpleNamespace(
         chain_names=tuple(chain_local), chain_local=tuple(chain_local.values()),
         helper_names=tuple(helper_local), helper_local=tuple(helper_local.values()),
         names=tuple(args) + tuple(outputs) + tuple(scratch),
         wide=wide, narrow=narrow, micros=micros, slots=slots,
         mid=mid, out=out, inw=inw, allch=allch,
-        starts=starts, layers=tuple(zip(starts, widths)), products=products,
+        gather=gather, layers=tuple(zip(starts, widths)), products=products,
     )
     results = pl.pallas_call(
         functools.partial(kernel, plan),

time: 140 us -> 114 us (0.81)
  Pallas kernels: 137 us -> 111 us
    pallas_call x1, Pallas kernels: 135 us -> 109 us  [shards(): pl.pallas_call(functools.partial(kernel, plan), out_shape=tuple((jax.Shap...]
where the time goes in v2:
time: 114 us; the launch traced here: 112 us
  Pallas kernels  111 us (97%)
    pallas_call x1, Pallas kernels, shards(): pl.pallas_call(functools.partial(kernel, plan), out_shape=tuple((jax.Shap...  109 us
    pallas_call x1, Pallas kernels, hand_out(): pl.pallas_call(copies, out_shape=tuple((jax.ShapeDtypeStruct(v.shape, v.d...  2.68 us

profile of v2, /device:TPU:11, one launch (start us, length us, event | category | flops | bytes accessed | tf_op | source)
XLA Modules:
  0.0 112.3 jit_solution(3045737600234235585)
XLA Ops:
  0.6 108.8 %bottleneck_pair.1 = (bf16[3,1,49,512]{3,2,1,0:T(8,128)(2,1)}, bf16[3,1,196,256]{3,2,1,0:T(8,128)(2,1)}, f32[128,128]{1,0:T(8,128)}, f32[9,64,128]{2,1,0:T(8,128...) custom-call(bf16[3,1,196,1024]{3,2,1,0:T(8,128)(2,1)} %refs_0_.1, ...), custom_call_target="tpu_custom_call" | custom-call | tf_op jit(solution)/shard_map/bottleneck_pair/pallas_call | solution.py:1262
  109.4 2.7 %hand_out.1 = (bf16[3,1,49,512]{3,2,1,0:T(8,128)(2,1)}, bf16[3,1,196,256]{3,2,1,0:T(8,128)(2,1)}, f32[128,128]{1,0:T(8,128)}, f32[9,64,128]{2,1,0:T(8,128)}, f32...) custom-call(bf16[3,1,49,512]{3,2,1,0:T(8,128)(2,1)} %get-tuple-eleme, ...), custom_call_target="tpu_custom_call" | custom-call | tf_op jit(solution)/shard_map/hand_out/pallas_call | solution.py:1052

commit v3 on v2

--- a/solution.py
+++ b/solution.py
@@ -23,7 +23,7 @@
 TAPS = 9
 STEPS = 15
 LOW_STEPS = (6, 7, 8, 9, 10, 11, 13)
-HALVING = ("e2", "r2", "e1", "p1")
+HALVING = ("p1",)
 
 
 def dot(a, b):
@@ -416,19 +416,14 @@
             side = r.image_sides[0, micro_of(s)]
             area = jnp.full((1, mid), side * side, jnp.int32).astype(F32)
             put(0, 2 * slots + s, area)
+        build_picks()
         pass_barrier()
         send_stats(0)
-        build_picks()
         for s in range(slots):
             build_tiles(s, micro_of(s))
         centre = r.pick[4 * HR : 5 * HR, :]
         for s in range(slots):
             r.picked[s * HR : (s + 1) * HR, :] = dot(centre, r.image[s]).astype(BF16)
-        fetch_weight(2).wait()
-        set_rows(r.z_short, dot(r.picked[...], r.k_project1[...]))
-        for s in range(slots):
-            put_pair(12, s, r.z_short[s])
-        send_stats(12)
         fetch_weight(1).wait()
         wait_stats(0)
         for s in range(slots):
@@ -446,6 +441,11 @@
             put_pair(1, s, rows_of(z, s) * half_wide(s, mid))
         send_stats(1)
         share(r.act1, r.h_act1.at[own_act], r.h_recv.at[0])
+        fetch_weight(2).wait()
+        set_rows(r.z_short, dot(r.picked[...], r.k_project1[...]))
+        for s in range(slots):
+            put_pair(12, s, r.z_short[s])
+        send_stats(12)
         for s in range(slots):
             r.slope0[s] = gelu_slope(activation(s, 0, r.z0[s])) * spread(r.full[s], mid)
         fetch_weight(3).wait()
@@ -725,7 +725,9 @@
 
     def wait_products():
         for index, spec in enumerate(plan.products):
-            wait_bytes(getattr(r, "out_" + spec.name), r.w_recv.at[index])
+            landing = getattr(r, "d_" + spec.name)
+            wait_bytes(landing, r.w_recv.at[index])
+            getattr(r, "out_" + spec.name)[...] = landing[...].astype(F32)
 
     def helper(*local):
         r.__dict__.update(zip(plan.helper_names, local))
@@ -889,13 +891,24 @@
                 wait_bytes(target, r.two_recv.at[index])
             elif places > 1:
                 wait_bytes(target.at[0 : places - 1], r.two_recv.at[index])
+            result = getattr(r, "out_" + spec.name)
+            landing = getattr(r, "d_" + spec.name)
+
+            def keep(half, part, at=Ellipsis):
+                last[(half,) if at is Ellipsis else (half, at)] = part.astype(BF16)
+                if half == 0:
+
+                    @pl.when(parity == 0)
+                    def _():
+                        result[at] = part
+
             if spec.gathered:
                 cols = getattr(r, "cols_" + spec.name)
                 value = dot_tn(flat(target[...]), cols[...])
                 for t in range(TAPS):
                     tap = value[:, t * 128 : (t + 1) * 128].T
                     for half in range(2):
-                        last[half, t] = tap[half * rows : (half + 1) * rows]
+                        keep(half, tap[half * rows : (half + 1) * rows], t)
             else:
                 if spec.halving:
                     value = getattr(r, "p_" + spec.name)[high, low].astype(F32)
@@ -907,17 +920,12 @@
                         value = value + target[q].astype(F32)
                 for half in range(2):
                     part = value[:, half * rows : (half + 1) * rows]
-                    last[half] = part if spec.taps > 1 else part[0]
-            result = getattr(r, "out_" + spec.name)
-
-            @pl.when(parity == 0)
-            def _():
-                result[...] = last[0]
+                    keep(half, part if spec.taps > 1 else part[0])
 
             sem = r.w_recv.at[index]
-            group.remote(last.at[1], result, sem, (partner, n), parity == 0)
-            group.remote(last.at[0], result, sem, (partner, n + 1), parity == 1)
-            group.remote(last.at[1], result, sem, (w, n + 1), parity == 1)
+            group.remote(last.at[1], landing, sem, (partner, n), parity == 0)
+            group.remote(last.at[0], landing, sem, (partner, n + 1), parity == 1)
+            group.remote(last.at[1], landing, sem, (w, n + 1), parity == 1)
 
         for m in range(micros):
             fetch_image(m, m).start()
@@ -981,21 +989,18 @@
         arrived(r.h_mix2, 6)
 
         start(0)
-        middle(0)
         start(1)
         start(2)
-        middle(2)
         start(4)
         start(3)
         middle(4)
-        middle(3)
         start(5)
-        start(6)
         finish(0)
         finish(1)
         finish(2)
+        start(6)
+        finish(3)
         finish(4)
-        finish(3)
         finish(5)
         finish(6)
 
@@ -1223,7 +1228,8 @@
                 scratch["two_" + name] = vmem((places,) + block, BF16)
                 helper_local["p_" + name] = vmem((places,) + block, BF16)
         last = (2, rows, width) if taps == 1 else (2, taps, rows, width)
-        helper_local["last_" + name] = vmem(last, F32)
+        helper_local["last_" + name] = vmem(last, BF16)
+        scratch["d_" + name] = vmem(last[1:], BF16)
     semaphores = dict(
         fetch=(16,),
         stat_send=(STEPS,),
@@ -1241,7 +1247,7 @@
     )
     for name, shape in semaphores.items():
         scratch[name] = pltpu.SemaphoreType.DMA(shape)
-    shared = ("h_", "o_", "sp", "ga", "cu", "on", "tw")
+    shared = ("h_", "o_", "sp", "ga", "cu", "on", "tw", "d_")
     chain_local = {name: scratch.pop(name) for name in tuple(scratch)
                    if name not in semaphores and name[:2] not in shared and name[:4] != "stat"}
     chain_local.update(

time: 114 us -> 106 us (0.930); the launches traced: 112 us -> 106 us
  Pallas kernels: 111 us -> 105 us
    pallas_call x1, Pallas kernels: 109 us -> 102 us  [shards(): pl.pallas_call(functools.partial(kernel, plan), out_shape=tuple((jax.Shap...]
where the time goes in v3:
time: 106 us
  Pallas kernels  105 us (99%)
    pallas_call x1, Pallas kernels, shards(): pl.pallas_call(functools.partial(kernel, plan), out_shape=tuple((jax.Shap...  102 us
    pallas_call x1, Pallas kernels, hand_out(): pl.pallas_call(copies, out_shape=tuple((jax.ShapeDtypeStruct(v.shape, v.d...  2.68 us

profile of v3, /device:TPU:11, one launch (start us, length us, event | category | flops | bytes accessed | tf_op | source)
XLA Modules:
  0.0 105.6 jit_solution(16273807179411717602)
XLA Ops:
  0.6 102.1 %bottleneck_pair.1 = (bf16[3,1,49,512]{3,2,1,0:T(8,128)(2,1)}, bf16[3,1,196,256]{3,2,1,0:T(8,128)(2,1)}, f32[128,128]{1,0:T(8,128)}, f32[9,64,128]{2,1,0:T(8,128...) custom-call(bf16[3,1,196,1024]{3,2,1,0:T(8,128)(2,1)} %refs_0_.1, ...), custom_call_target="tpu_custom_call" | custom-call | tf_op jit(solution)/shard_map/bottleneck_pair/pallas_call | solution.py:1268
  102.7 2.7 %hand_out.1 = (bf16[3,1,49,512]{3,2,1,0:T(8,128)(2,1)}, bf16[3,1,196,256]{3,2,1,0:T(8,128)(2,1)}, f32[128,128]{1,0:T(8,128)}, f32[9,64,128]{2,1,0:T(8,128)}, f32...) custom-call(bf16[3,1,49,512]{3,2,1,0:T(8,128)(2,1)} %get-tuple-eleme, ...), custom_call_target="tpu_custom_call" | custom-call | tf_op jit(solution)/shard_map/hand_out/pallas_call | solution.py:1057

commit v4 on v3

--- a/solution.py
+++ b/solution.py
@@ -377,7 +377,8 @@
             dst = getattr(r, "h_g_" + spec.name)
             for c in range(columns):
                 amount = min(slots, micros - c * slots)
-                for quarter in range(narrow if amount > 0 else 0):
+                order = sorted(range(narrow), key=lambda quarter: quarter // 2 == c)
+                for quarter in order if amount > 0 else ():
                     h, v = quarter // 2, quarter % 2
                     group.remote(
                         src.at[0:amount, :, quarter * spec.width : (quarter + 1) * spec.width],
@@ -633,8 +634,8 @@
             k0, k1, k2 = settle_back(s, 3, 13, sums_u[s], low_total(13, s, slots))
             grad = (k0 * r.u_out[s] + k1 + k2 * r.z_short[s]) * half_wide(s, out)
             r.g_p1[s] = grad.astype(BF16)
+        share_grad(r.g_e1, 3)
         share_grad(r.g_p1, 4)
-        share_grad(r.g_e1, 3)
         build_pick_back()
         r.picked[...] = dot_nt(rows2(r.g_p1), r.k_project1[...]).astype(
             BF16

time: 106 us -> 106 us (level)
  no operation moved by 1% of the time
where the time goes in v4:
time: 106 us
  Pallas kernels  105 us (99%)
    pallas_call x1, Pallas kernels, shards(): pl.pallas_call(functools.partial(kernel, plan), out_shape=tuple((jax.Shap...  102 us
    pallas_call x1, Pallas kernels, hand_out(): pl.pallas_call(copies, out_shape=tuple((jax.ShapeDtypeStruct(v.shape, v.d...  2.68 us

profile of v4, /device:TPU:11, one launch (start us, length us, event | category | flops | bytes accessed | tf_op | source)
XLA Modules:
  0.0 105.6 jit_solution(3839133310645094758)
XLA Ops:
  0.6 102.1 %bottleneck_pair.1 = (bf16[3,1,49,512]{3,2,1,0:T(8,128)(2,1)}, bf16[3,1,196,256]{3,2,1,0:T(8,128)(2,1)}, f32[128,128]{1,0:T(8,128)}, f32[9,64,128]{2,1,0:T(8,128...) custom-call(bf16[3,1,196,1024]{3,2,1,0:T(8,128)(2,1)} %refs_0_.1, ...), custom_call_target="tpu_custom_call" | custom-call | tf_op jit(solution)/shard_map/bottleneck_pair/pallas_call | solution.py:1269
  102.7 2.7 %hand_out.1 = (bf16[3,1,49,512]{3,2,1,0:T(8,128)(2,1)}, bf16[3,1,196,256]{3,2,1,0:T(8,128)(2,1)}, f32[128,128]{1,0:T(8,128)}, f32[9,64,128]{2,1,0:T(8,128)}, f32...) custom-call(bf16[3,1,49,512]{3,2,1,0:T(8,128)(2,1)} %get-tuple-eleme, ...), custom_call_target="tpu_custom_call" | custom-call | tf_op jit(solution)/shard_map/hand_out/pallas_call | solution.py:1058
